TPU v7x, 512 devices: a whole 4x8x8 slice. The times are simulated.
512 devices in a mesh: ctx: 64 (over x, y, core), ch: 8 (over z).
Axes of the slice: x: 4, y: 8, z: 8, core: 2. Of those that a mesh axis runs over, the one named last changes fastest.
Arguments:
- features: bfloat16 [10240, 3, 4096], P('ctx', None, 'ch'), may hold values from -6 to 6
- segment_ids: int32 [10240], P('ctx'), may hold values from 0 to 63, never falling along the last dimension, each value on 1 to 320 neighbouring positions
- feat_taps: float32 [3, 3, 4096], P(None, None, 'ch'), may hold values from -3 to 3
- mixer_filter: float32 [256, 128], P('ch'), may hold values from -0.5 to 0.5
- skip_gain: float32 [4096], P('ch'), may hold values from 0.5 to 1.5
- out_weight: bfloat16 [4096, 8192], P('ctx', 'ch'), may hold values from -0.09375 to 0.09375
- targets: int32 [10240], P('ctx'), may hold values from 0 to 63, as said below
- row_costs: int32 [10240], P('ctx'), may hold values from 1 to 160
Outputs:
- relaid_out: bfloat16 [10240, 8192], P('ctx', 'ch')
- shard_cost: float32 [64], P('ctx')
Inputs may be any that keep to these rules, and one draw needn't show every extreme that they name: `segment_ids`: never fall along the rows. `targets`: each shard sends exactly 5 of its rows to each of 32 target shards and none to the others; every shard receives exactly 160 rows.
All inputs are finite; a program needn't handle non-finite values.
Results may differ from a plain program's by a relative error of at most 0.014.
Values may be sent and summed in bfloat16 or wider, within the bound.
A program may use at most 64 MiB of HBM per device.

v0:
```python
import math

import jax
import jax.numpy as jnp
from jax import lax
from jax.sharding import PartitionSpec as P


def passed_along(x, axis, by):
    size = lax.axis_size(axis)
    pairs = [(i, i + by) for i in range(size) if 0 <= i + by < size]
    return lax.ppermute(x, axis, pairs)


def short_filter(extended, extended_seg, tap_weights):
    center = extended[2:].astype(jnp.float32)
    one_back = extended[1:-1].astype(jnp.float32)
    two_back = extended[:-2].astype(jnp.float32)
    match_one = (extended_seg[2:] == extended_seg[1:-1]).astype(jnp.float32)[:, None, None]
    match_two = (extended_seg[2:] == extended_seg[:-2]).astype(jnp.float32)[:, None, None]
    return (
        tap_weights[:, 0, :][None] * center
        + tap_weights[:, 1, :][None] * one_back * match_one
        + tap_weights[:, 2, :][None] * two_back * match_two
    )


def relay_rows(row_block, targets, row_costs):
    shards = lax.axis_size("ctx")
    row_count = row_block.shape[0]
    capacity = 2 * row_count // shards
    onehot = (targets[:, None] == jnp.arange(shards, dtype=jnp.int32)[None, :]).astype(jnp.int32)
    before = jnp.cumsum(onehot, axis=0) - onehot
    slot_rank = jnp.sum(before * onehot, axis=1)
    counts = jnp.sum(onehot, axis=0)
    slot_index = targets * capacity + slot_rank
    source = (
        jnp.zeros((shards * capacity,), jnp.int32)
        .at[slot_index]
        .set(jnp.arange(row_count, dtype=jnp.int32))
    )
    filled = jnp.zeros((shards * capacity,), jnp.bool_).at[slot_index].set(True)
    packed = jnp.where(filled[:, None], row_block[source], jnp.zeros((), row_block.dtype))
    packed_cost = jnp.where(filled, row_costs[source], 0)
    arrived, arrived_cost, arrived_counts = (
        lax.all_to_all(packed, "ctx", split_axis=0, concat_axis=0, tiled=True),
        lax.all_to_all(packed_cost, "ctx", split_axis=0, concat_axis=0, tiled=True),
        lax.all_to_all(counts, "ctx", split_axis=0, concat_axis=0, tiled=True),
    )
    offsets = jnp.cumsum(arrived_counts) - arrived_counts
    slot_ids = jnp.arange(shards * capacity, dtype=jnp.int32)
    within = slot_ids % capacity
    sender = slot_ids // capacity
    is_live = within < arrived_counts[sender]
    target_row = jnp.where(is_live, offsets[sender] + within, row_count)
    placed = (
        jnp.zeros((row_count + 1, row_block.shape[1]), row_block.dtype)
        .at[target_row]
        .set(arrived)[:row_count]
    )
    total_cost = jnp.sum(jnp.where(is_live, arrived_cost, 0))
    return (placed, total_cost)


def project(gated_rows, out_weight):
    all_channels = lax.all_gather(gated_rows, "ch", axis=1, tiled=True)
    summed = jnp.dot(
        all_channels,
        lax.all_gather(out_weight, "ctx", axis=0, tiled=True),
        preferred_element_type=jnp.float32,
    )
    return summed.astype(jnp.bfloat16)


def local(
    features, segment_ids, feat_taps, mixer_filter, skip_gain, out_weight, targets, row_costs
):
    length = features.shape[0]
    width = features.shape[2]
    tap_count = mixer_filter.shape[1]
    groups = mixer_filter.shape[0]
    coded_seg = segment_ids + 1
    rim_rows, rim_seg = passed_along((features[length - 2 :], coded_seg[length - 2 :]), "ctx", 1)
    featured = short_filter(
        jnp.concatenate([rim_rows, features], axis=0),
        jnp.concatenate([rim_seg, coded_seg]),
        feat_taps,
    )
    mixer_in = (featured[:, 1] * featured[:, 2]).astype(jnp.bfloat16)
    tail_in, tail_seg = passed_along(
        (mixer_in[length - tap_count + 1 :], coded_seg[length - tap_count + 1 :]), "ctx", 1
    )
    extended = jnp.concatenate([jnp.zeros((1, width), jnp.bfloat16), tail_in, mixer_in], axis=0)
    extended_seg = jnp.concatenate([jnp.zeros((1,), jnp.int32), tail_seg, coded_seg])
    block_rows = math.gcd(length, 128)
    filter_half = mixer_filter.astype(jnp.bfloat16)
    row_ids = jnp.arange(block_rows, dtype=jnp.int32)
    column_ids = jnp.arange(block_rows + tap_count, dtype=jnp.int32)
    lag_table = tap_count + row_ids[:, None] - column_ids[None, :]
    in_reach = (lag_table >= 0) & (lag_table < tap_count)
    toeplitz = jnp.where(
        in_reach[None],
        jnp.take(filter_half, jnp.clip(lag_table, 0, tap_count - 1), axis=1),
        jnp.zeros((), jnp.bfloat16),
    )
    block_outs = []
    for block_index in range(length // block_rows):
        first_row = block_index * block_rows
        window = extended[first_row : first_row + block_rows + tap_count]
        window_seg = extended_seg[first_row : first_row + block_rows + tap_count]
        row_seg = coded_seg[first_row : first_row + block_rows]
        same_segment = row_seg[:, None] == window_seg[None, :]
        matrix = jnp.where(same_segment[None], toeplitz, jnp.zeros((), jnp.bfloat16))
        block_out = jnp.einsum(
            "gts,sgc->tgc",
            matrix,
            window.reshape(block_rows + tap_count, groups, width // groups),
            preferred_element_type=jnp.float32,
        )
        block_outs.append(block_out.reshape(block_rows, width))
    filtered = jnp.concatenate(block_outs, axis=0)
    gated_rows = (
        featured[:, 0] * (filtered + skip_gain[None, :] * mixer_in.astype(jnp.float32))
    ).astype(jnp.bfloat16)
    projected = project(gated_rows, out_weight)
    relaid_out, total_cost = relay_rows(projected, targets, row_costs)
    shard_cost = (total_cost.astype(jnp.float32) / (32.0 * length)).reshape(1)
    return (relaid_out, shard_cost)


def solution(mesh):
    placed = (
        P("ctx", None, "ch"),
        P("ctx"),
        P(None, None, "ch"),
        P("ch", None),
        P("ch"),
        P("ctx", "ch"),
        P("ctx"),
        P("ctx"),
    )
    return jax.shard_map(
        local, mesh=mesh, in_specs=placed, out_specs=(P("ctx", "ch"), P("ctx")), check_vma=False
    )
```

profile of v0, /device:TPU:1, one launch (start us, length us, event | category | flops | bytes accessed | tf_op | source)
XLA Modules:
  0.0 302.0 jit_solution(1549635899773887766)
XLA Ops:
  7.2 0.7 broadcast_add_fusion
  8.0 4.6 %collective-permute-start.1 = (s32[2]{0:T(128)S(1)}, s32[2]{0:T(128)S(1)}, u32[]{:S(2)}, u32[]{:S(2)}) collective-permute-start(s32[2]{0:T(128)S(1)} %slice.109), channel_id=1, source_target_pairs={{0,8},{8,16},{16,24},{24,32},{32,40},{40,48},{48,56},{56,64},{64,7... | collective-permute-start | bytes 32 | tf_op jit(solution)/shard_map/ppermute | solution.py:12
  12.6 0.8 slice.107
  13.3 1.0 copy.58
  14.3 1.9 collective-permute-start
  16.3 3.6 %collective-permute-start.3 = (s32[127]{0:T(128)S(1)}, s32[127]{0:T(128)S(1)}, u32[]{:S(2)}, u32[]{:S(2)}) collective-permute-start(s32[127]{0:T(128)S(1)} %slice.121), channel_id=1, source_target_pairs={{0,8},{8,16},{16,24},{24,32},{32,40},{40,48},{48,56},{56,64},{64,7... | collective-permute-start | bytes 1532 | tf_op jit(solution)/shard_map/ppermute | solution.py:12
  19.9 1.3 copy.57
  21.3 0.1 fusion.41
  21.7 0.1 copy.60
  21.8 15.1 %gather_fusion = bf16[5120,32]{1,0:T(8,128)(2,1)S(1)} fusion(bf16[32,128]{0,1:T(8,128)(2,1)S(1)} %copy.60, s32[5120]{0:T(1024)S(1)} %broadcast_clamp_fusion), kind=kCustom, calls=%fused_computation | custom fusion | bytes 675840 | tf_op jit(solution)/shard_map/jit(_take)/gather | solution.py:103
  36.9 1.0 copy.61
  38.6 1.4 multiply_add_fusion
  40.0 0.1 slice_bitcast_fusion.1
  40.2 1.9 collective-permute-start.2
  42.1 0.3 fusion.3
  42.4 1.6 collective-permute-done.2
  44.0 0.5 pad_maximum_fusion.1
  44.5 0.3 fusion.7
  44.8 0.3 fusion.5
  45.1 0.3 fusion.9
  45.3 1.0 fusion.11
  46.3 0.3 concatenate.31
  46.6 0.9 fusion.2
  47.6 0.7 all-gather.5.cloned.1.call-update
  48.3 0.6 reduce-window.20
  48.9 0.2 slice_reduce_fusion
  49.2 0.1 bitcast_bitcast_fusion
  49.3 0.1 fusion.33
  49.4 0.7 copy.53
  50.1 11.7 %all-to-all-start = ((s32[64,1,1]{2,1,0:T(1,128)}), s32[64,1,1]{2,1,0:T(1,128)S(1)}, u32[]{:S(2)}, u32[]{:S(2)}) async-start(s32[64,1,1]{2,1,0:T(1,128)} %copy.53), calls=%async_computation | async-start | bytes 65536 | tf_op jit(solution)/shard_map/all_to_all | solution.py:48
  61.8 1.1 scatter_custom_fusion.1
  62.9 1.1 scatter_custom_fusion
  64.1 2.5 gather_fusion.2
  68.8 0.1 broadcast_in_dim.126
  68.9 0.7 all_to_all.25
  69.6 1.4 all-to-all-done
  71.1 8.9 %all-to-all-start.2 = ((s32[64,5,1]{1,2,0:T(1,128)}), s32[64,5,1]{1,2,0:T(1,128)S(1)}, u32[]{:S(2)}, u32[]{:S(2)}) async-start(s32[64,5,1]{1,2,0:T(1,128)} %bitcast.155), calls=%async_computation.2 | async-start | bytes 65536 | tf_op jit(solution)/shard_map/all_to_all | solution.py:47
  80.0 0.7 fusion.56
  80.7 13.2 %all-gather.3.cloned.1.call-done = bf16[160,4096]{0,1:T(8,128)(2,1)} async-done(((bf16[160,512]{0,1:T(8,128)(2,1)}), bf16[160,4096]{0,1:T(8,128)(2,1)}) %all-gather.3.cloned.1.call-update) | async-done | bytes 1310736 | tf_op jit(solution)/shard_map/all_gather | solution.py:66
  93.9 94.1 %all-gather.5.cloned.1.call-done = bf16[4096,1024]{1,0:T(8,128)(2,1)} async-done(((bf16[64,1024]{1,0:T(8,128)(2,1)}), bf16[4096,1024]{1,0:T(8,128)(2,1)}) %all-gather.5.cloned.1.call-update) | async-done | bytes 8388624 | tf_op jit(solution)/shard_map/all_gather | solution.py:69
  188.0 5.6 %convolution_convert_fusion = bf16[160,1024]{1,0:T(8,128)(2,1)S(1)} fusion(bf16[160,4096]{0,1:T(8,128)(2,1)} %all-gather.3.cloned.1.call-done, bf16[4096,1024]{1,0:T(8,128)(2,1)} %all-gather.5.cloned.1.call-done), kind=kOutput, calls=%fused_computation.7 | convolution fusion | flops 1342341120 | bytes 10027008 | tf_op jit(solution)/shard_map/dot_general | solution.py:67
  193.6 2.1 gather_fusion.1
  195.7 0.3 gather.30
  195.9 1.2 broadcast_select_fusion
  197.1 6.3 %all-to-all-start.1 = ((bf16[64,5,1024]{2,1,0:T(8,128)(2,1)}), bf16[64,5,1024]{2,1,0:T(8,128)(2,1)S(1)}, u32[]{:S(2)}, u32[]{:S(2)}) async-start(bf16[64,5,1024]{2,1,0:T(8,128)(2,1)} %broadcast_select_fusion), calls=%async_computation.1 | async-start | bytes 2097152 | tf_op jit(solution)/shard_map/all_to_all | solution.py:46
  203.4 0.6 fusion.59
  204.0 0.1 reduce-window.19
  204.1 0.1 reduce.59
  204.2 4.4 %fusion.45 = s32[320]{0:T(512)S(1)} fusion(s32[]{:T(128)} %bitcast.58, s32[]{:T(128)} %bitcast.59, s32[]{:T(128)} %bitcast.60, s32[]{:T(128)} %bitcast.61, s32[]{:T(128)} %bitcast.62, s32[]{:T(128)} %bitcast.64, s32[]{:T(128)} %bitcast.63), kind=kLoop, calls=%fused_computation.175 | loop fusion | flops 7360 | bytes 1308 | tf_op jit(solution)/shard_map/gather | solution.py:54
  208.6 0.7 fusion.58
  209.2 0.7 fusion.57
  209.9 35.5 %select_select_fusion.2 = s32[320]{0:T(512)S(1)} fusion(pred[320]{0:T(512)(128)(4,1)S(1)} %compare_reduce_fusion, pred[320]{0:T(512)(128)(4,1)S(1)} %compare_reduce_fusion.1, pred[320]{0:T(512)(128)(4,1)S(1)} %compare_reduce_fusion.2, pred[320]{0:T(512)(128)(4,1)S(1)} %compare_reduce_fusion.3, pred[320]{0:T(512)(128)(4,1)S(1)} %compare_reduce_fusion.4, ...), kind=kLoop, calls=%fused_computation.171 | loop fusion | flops 18240 | bytes 21028 | tf_op jit(solution)/shard_map/gather | solution.py:54
  245.4 0.1 gather.31
  245.5 1.2 reduce.60
  246.7 0.7 fusion.66
  247.4 0.7 fusion.65
  248.1 4.4 %fusion.44 = s32[320]{0:T(512)S(1)} fusion(s32[]{:T(128)} %bitcast.123, s32[]{:T(128)} %bitcast.124, s32[]{:T(128)} %bitcast.125, s32[]{:T(128)} %bitcast.126, s32[]{:T(128)} %bitcast.127, s32[]{:T(128)} %bitcast.129, s32[]{:T(128)} %bitcast.128), kind=kLoop, calls=%fused_computation.174 | loop fusion | flops 7360 | bytes 1308 | tf_op jit(solution)/shard_map/gather | solution.py:55
  252.5 0.7 fusion.64
  253.3 0.7 fusion.63
  254.0 35.7 %select_select_fusion.1 = s32[320]{0:T(512)S(1)} fusion(pred[320]{0:T(512)(128)(4,1)S(1)} %compare_reduce_fusion, pred[320]{0:T(512)(128)(4,1)S(1)} %compare_reduce_fusion.1, pred[320]{0:T(512)(128)(4,1)S(1)} %compare_reduce_fusion.2, pred[320]{0:T(512)(128)(4,1)S(1)} %compare_reduce_fusion.3, pred[320]{0:T(512)(128)(4,1)S(1)} %compare_reduce_fusion.4, ...), kind=kLoop, calls=%fused_computation.170 | loop fusion | flops 18240 | bytes 21028 | tf_op jit(solution)/shard_map/gather | solution.py:55
  289.7 0.7 select_reduce_fusion
  291.0 0.3 reshape.646
  291.3 2.0 scatter_custom_fusion.2
  293.3 0.7 slice.412
  (115 shorter events, 3.6 us)
Async XLA Ops:
  7.2 56.9 %copy-start = (s32[160]{0:T(256)S(1)}, s32[160]{0:T(256)}, u32[]{:S(2)}) copy-start(s32[160]{0:T(256)} %param.15) | copy-start | bytes 1924
  7.2 14.3 %copy-start.2 = (f32[3,3,512]{2,1,0:T(4,128)S(1)}, f32[3,3,512]{2,1,0:T(4,128)}, u32[]{:S(2)}) copy-start(f32[3,3,512]{2,1,0:T(4,128)} %param.10) | copy-start | bytes 55300
  7.2 14.4 %copy-start.1 = (f32[32,128]{1,0:T(8,128)S(1)}, f32[32,128]{1,0:T(8,128)}, u32[]{:S(2)}) copy-start(f32[32,128]{1,0:T(8,128)} %param.11) | copy-start | bytes 49156
  7.2 86.7 %all-gather.3.cloned.1.call-start = ((), (), s32[]{:S(2)}) async-start(), calls=%async_computation.3 | async-start | bytes 2359296 | tf_op jit(solution)/shard_map/all_gather | solution.py:66
  8.0 30.0 %collective-permute-start.1 = (s32[2]{0:T(128)S(1)}, s32[2]{0:T(128)S(1)}, u32[]{:S(2)}, u32[]{:S(2)}) collective-permute-start(s32[2]{0:T(128)S(1)} %slice.109), channel_id=1, source_target_pairs={{0,8},{8,16},{16,24},{24,32},{32,40},{40,48},{48,56},{56,64},{64,7... | collective-permute-start | bytes 32 | tf_op jit(solution)/shard_map/ppermute | solution.py:12
  14.3 24.3 %collective-permute-start = (bf16[2,3,512]{0,2,1:T(8,128)(2,1)}, bf16[2,3,512]{0,2,1:T(8,128)(2,1)S(1)}, u32[]{:S(2)}, u32[]{:S(2)}) collective-permute-start(bf16[2,3,512]{0,2,1:T(8,128)(2,1)} %copy.58), channel_id=1, source_target_pairs={{0,8},{8,16},{16,24},{24,32},{32,40},{40,48},{48,56},{56,64},{64,7... | collective-permute-start | bytes 18440 | tf_op jit(solution)/shard_map/ppermute | solution.py:12
  16.3 21.9 %collective-permute-start.3 = (s32[127]{0:T(128)S(1)}, s32[127]{0:T(128)S(1)}, u32[]{:S(2)}, u32[]{:S(2)}) collective-permute-start(s32[127]{0:T(128)S(1)} %slice.121), channel_id=1, source_target_pairs={{0,8},{8,16},{16,24},{24,32},{32,40},{40,48},{48,56},{56,64},{64,7... | collective-permute-start | bytes 1532 | tf_op jit(solution)/shard_map/ppermute | solution.py:12
  21.4 23.7 %copy-start.4 = (pred[32,160]{1,0:T(8,128)(4,1)}, pred[32,160]{1,0:T(8,128)(4,1)S(1)}, u32[]{:S(2)}) copy-start(pred[32,160]{1,0:T(8,128)(4,1)S(1)} %get-tuple-element.86) | copy-start | bytes 15364
  36.9 1.2 copy-start.5
  40.2 3.9 %collective-permute-start.2 = (bf16[127,512]{0,1:T(8,128)(2,1)S(1)}, bf16[127,512]{0,1:T(8,128)(2,1)S(1)}, u32[]{:S(2)}, u32[]{:S(2)}) collective-permute-start(bf16[127,512]{0,1:T(8,128)(2,1)S(1)} %slice_bitcast_fusion.1), channel_id=1, source_target_pairs={{0,8},{8,16},{16,24},{24,32},{32,40},{40,48},{48,56},{56,64},{64,7... | collective-permute-start | bytes 390152 | tf_op jit(solution)/shard_map/ppermute | solution.py:12
  45.3 1.3 copy-start.6
  46.6 1.6 copy-start.3
  47.5 140.5 %all-gather.5.cloned.1.call-start = ((), (), s32[]{:S(2)}) async-start(), calls=%async_computation.4 | async-start | bytes 8519680 | tf_op jit(solution)/shard_map/all_gather | solution.py:69
  50.1 21.0 %all-to-all-start = ((s32[64,1,1]{2,1,0:T(1,128)}), s32[64,1,1]{2,1,0:T(1,128)S(1)}, u32[]{:S(2)}, u32[]{:S(2)}) async-start(s32[64,1,1]{2,1,0:T(1,128)} %copy.53), calls=%async_computation | async-start | bytes 65536 | tf_op jit(solution)/shard_map/all_to_all | solution.py:48
  71.1 126.0 %all-to-all-start.2 = ((s32[64,5,1]{1,2,0:T(1,128)}), s32[64,5,1]{1,2,0:T(1,128)S(1)}, u32[]{:S(2)}, u32[]{:S(2)}) async-start(s32[64,5,1]{1,2,0:T(1,128)} %bitcast.155), calls=%async_computation.2 | async-start | bytes 65536 | tf_op jit(solution)/shard_map/all_to_all | solution.py:47
  197.1 93.9 %all-to-all-start.1 = ((bf16[64,5,1024]{2,1,0:T(8,128)(2,1)}), bf16[64,5,1024]{2,1,0:T(8,128)(2,1)S(1)}, u32[]{:S(2)}, u32[]{:S(2)}) async-start(bf16[64,5,1024]{2,1,0:T(8,128)(2,1)} %broadcast_select_fusion), calls=%async_computation.1 | async-start | bytes 2097152 | tf_op jit(solution)/shard_map/all_to_all | solution.py:46
Sparse Core Ops, SparseCore 0:
  47.6 46.1 all-gather.2
  97.2 90.7 all-gather.4
where the time goes:
time: 304 us; the launch traced here: 302 us
  waiting for transfers between devices  111 us (37%)
  other arithmetic  90.5 us (30%)
  starting transfers between devices  38.9 us (13%)
  local copies, waits for them, and re-layouts  37.5 us (12%)
  between operations  16.4 us (5%)
  matrix products  7.53 us (2%)
    all_gather x1, waiting for transfers between devices, project(): lax.all_gather(out_weight, 'ctx', axis=0, tiled=True)  94.1 us
    gather x59, other arithmetic, relay_rows(): is_live = within < arrived_counts[sender]  42 us
    gather x2, other arithmetic, relay_rows(): target_row = jnp.where(is_live, offsets[sender] + within, row_count)  40.1 us
    gather x2, local copies, waits for them, and re-layouts, local(): jnp.take(filter_half, jnp.clip(lag_table, 0, tap_count - 1), axis=1)  16.1 us
    all_gather x1, waiting for transfers between devices, project(): all_channels = lax.all_gather(gated_rows, 'ch', axis=1, tiled=True)  13.2 us
    ppermute x4, starting transfers between devices, passed_along(): return lax.ppermute(x, axis, pairs)  12 us
    all_to_all x1, starting transfers between devices, relay_rows(): lax.all_to_all(counts, 'ctx', split_axis=0, concat_axis=0, tiled=True)  11.7 us
    all_to_all x1, starting transfers between devices, relay_rows(): lax.all_to_all(packed_cost, 'ctx', split_axis=0, concat_axis=0, tiled=True)  8.91 us
  transfers between devices with their start and end apart: 9, of which 4 were waited for; matrix products, arithmetic and copies ran while one was open for 42% of the time, Pallas kernels for 0%

commit v1 on v0

v1 whole, which is shorter than its diff:
```python
import functools

import jax
import jax.numpy as jnp
from jax import lax
from jax.experimental import pallas as pl
from jax.experimental.pallas import tpu as pltpu
from jax.sharding import PartitionSpec as P

MESH = pl.DeviceIdType.MESH
BF = jnp.bfloat16
F32 = jnp.float32
ROWS = 160
TAPS = 128
UNITS = 2
ACOLS = 128
BCOLS = 384


def place():
    ctx = lax.axis_index("ctx")
    return ctx // 16, (ctx // 2) % 8, ctx % 2, lax.axis_index("ch"), ctx


def offset_of(j):
    return ((j + 1) // 2) * (2 * (j % 2) - 1)


def iota(shape, dim):
    return lax.broadcasted_iota(jnp.int32, shape, dim)


def mixer_kernel(
    feat_in, w_in, taps, filt, gain, meta, metac,
    out, cost_out,
    feat, qf, win, hrev, mask_s, gsend, gbuf, cbuf, slots, prevmeta,
    packed, arrived, dmat, abuf, wa, wb, acc, osend, orecv,
    s_feat, s_loc, s_sib, r_sib, s_halo, r_halo, s_gx, r_gx, s_rel, r_rel, s_self,
    s_ax, r_ax, s_ay, r_ay, s_by, r_by, s_bx, r_bx, s_bx2, r_bx2,
    s_z, r_z, s_c, r_c, s_o, r_o,
):
    x, y, k, z, ctx = place()
    chip = x * 8 + y
    kk = 1 - k

    def dev(dx=0, dy=0, dz=0, dk=0):
        return (
            (((x + dx + 4) % 4) * 8 + (y + dy + 8) % 8) * 2 + (k + dk) % 2,
            (z + dz + 8) % 8,
        )

    sibling = dev(dk=1)
    following = ((ctx + 1) % 64, z)
    previous = ((ctx + 63) % 64, z)
    pending = []

    def send(src, dst, ssem, rsem, to):
        c = pltpu.make_async_remote_copy(
            src_ref=src, dst_ref=dst, send_sem=ssem, recv_sem=rsem,
            device_id=to, device_id_type=MESH,
        )
        c.start()
        pending.append(c)

    def arrived_at(dst, ssem, rsem):
        pltpu.make_async_remote_copy(
            src_ref=dst, dst_ref=dst, send_sem=ssem, recv_sem=rsem,
            device_id=sibling, device_id_type=MESH,
        ).wait_recv()

    load = pltpu.make_async_copy(feat_in, feat.at[:, pl.ds(16, ROWS)], s_feat)
    load.start()
    barrier = pltpu.get_barrier_semaphore()

    def greet(i, carry):
        other = (chip + i) % 32
        pl.semaphore_signal(barrier, inc=1, device_id=(other * 2 + k, z), device_id_type=MESH)
        return carry

    lax.fori_loop(1, 32, greet, 0)
    for to in (sibling, following, previous, dev(dz=1), dev(dz=-1)):
        pl.semaphore_signal(barrier, inc=1, device_id=to, device_id_type=MESH)

    own_a = wa.at[y, x]
    own_b = wb.at[x, y]
    mine = pl.ds(pl.multiple_of(k * 64, 64), 64)

    def wcols(core, first, count):
        return w_in.at[:, pl.ds(pl.multiple_of(core * 512 + first, 128), count)]

    loc_a = pltpu.make_async_copy(wcols(k, 0, ACOLS), own_a.at[mine], s_loc.at[0])
    loc_b = pltpu.make_async_copy(wcols(k, ACOLS, BCOLS), own_b.at[mine], s_loc.at[1])
    loc_a.start()
    loc_b.start()

    seg_col = metac[:, 0:1]
    tgt_col = metac[:, 1:2]
    cost_col = metac[:, 2:3]
    lag = iota((ROWS, 384), 0) + TAPS - iota((ROWS, 384), 1)
    in_reach = (lag >= 0) & (lag < TAPS)

    def same_segment(prev_row):
        seg_row = jnp.concatenate([prev_row, meta[0:1, :]], axis=1)
        return jnp.where(in_reach & (seg_col == seg_row), 1.0, 0.0)

    def featurize(index, center, match_one, match_two):
        return (
            taps[index, 0:1, :] * center
            + taps[index, 1:2, :] * pltpu.roll(center, 1, 0) * match_one
            + taps[index, 2:3, :] * pltpu.roll(center, 2, 0) * match_two
        )

    seg_own = same_segment(jnp.full((1, 128), -1.0, F32))
    back = jnp.sum(seg_own, axis=1, keepdims=True)
    m_one = jnp.where(back > 1.5, 1.0, 0.0)
    m_two = jnp.where(back > 2.5, 1.0, 0.0)
    load.wait()
    own_rows = pl.ds(16, ROWS)
    qf[...] = featurize(0, feat[0, own_rows].astype(F32), m_one, m_two)
    win[pl.ds(128, ROWS), :] = (
        featurize(1, feat[1, own_rows].astype(F32), m_one, m_two)
        * featurize(2, feat[2, own_rows].astype(F32), m_one, m_two)
    ).astype(BF)
    win[pl.ds(288, 96), :] = jnp.zeros((96, 512), BF)

    tgt_row = meta[1:2, :]
    same_target = tgt_col == tgt_row
    rq = iota((ROWS, 256), 0)
    rr = iota((ROWS, 256), 1)
    rank_row = jnp.sum(jnp.where(same_target & (rq < rr), 1.0, 0.0), axis=0, keepdims=True)
    rank_col = jnp.sum(jnp.where(same_target & (rr < rq), 1.0, 0.0), axis=1, keepdims=True)
    kf = k.astype(F32)
    chip_row = jnp.floor(tgt_row * 0.5)
    chip_col = jnp.floor(tgt_col * 0.5)
    lane_row = (tgt_row - 2.0 * chip_row) * 10.0 + kf * 5.0 + rank_row
    lane_col = (tgt_col - 2.0 * chip_col) * 10.0 + kf * 5.0 + rank_col
    slots[k, 0:1, :] = chip_row * 32.0 + lane_row
    slots[k, 1:2, :] = chip_row * 32.0 + 20.0
    mine_rows = pl.ds(pl.multiple_of(k * ROWS, 16), ROWS)
    cbuf[mine_rows, :] = jnp.where(
        iota((ROWS, 128), 1).astype(F32) == lane_col, cost_col, 0.0
    ).astype(BF)

    flip = (iota((TAPS, TAPS), 0) + iota((TAPS, TAPS), 1)) % TAPS == 0
    hrev[...] = jnp.dot(
        filt[...].astype(BF), jnp.where(flip, 1.0, 0.0).astype(BF), preferred_element_type=F32
    )

    pl.semaphore_wait(barrier, 36)

    send(wcols(kk, 0, ACOLS), own_a.at[mine], s_sib.at[0], r_sib.at[0], sibling)
    send(wcols(kk, ACOLS, BCOLS), own_b.at[mine], s_sib.at[1], r_sib.at[1], sibling)
    send(feat.at[:, pl.ds(160, 16)], feat.at[:, pl.ds(0, 16)], s_halo.at[0], r_halo.at[0], following)
    send(meta, prevmeta, s_halo.at[1], r_halo.at[1], following)
    send(win.at[pl.ds(160, 128)], win.at[pl.ds(0, 128)], s_halo.at[2], r_halo.at[2], following)
    send(slots.at[k], slots.at[k], s_gx.at[1], r_gx.at[1], sibling)
    send(cbuf.at[mine_rows], cbuf.at[mine_rows], s_gx.at[2], r_gx.at[2], sibling)

    events = []

    def at(when, what, *args):
        events.append((when, len(events), functools.partial(what, *args)))

    def w_own():
        theirs = pl.ds(pl.multiple_of(kk * 64, 64), 64)
        loc_a.wait()
        loc_b.wait()
        arrived_at(own_a.at[theirs], s_sib.at[0], r_sib.at[0])
        arrived_at(own_b.at[theirs], s_sib.at[1], r_sib.at[1])
        for d in (1, 2, 3):
            send(own_a, own_a, s_ax.at[d - 1], r_ax.at[d - 1], dev(dx=d))
        by_send(1)
        bx_send(0)

    def by_piece(t, way):
        ref = wb.at[x, (y + (1 - t if way == 0 else t - 1) + 8) % 8]
        return ref if t < 4 else ref.at[pl.ds(way * 64, 64)]

    def by_landed(t, way):
        ref = wb.at[x, (y + (-t if way == 0 else t) + 8) % 8]
        return ref if t < 4 else ref.at[pl.ds(way * 64, 64)]

    def by_send(t):
        for way in (0, 1):
            piece = by_piece(t, way)
            send(piece, piece, s_by.at[way, t - 1], r_by.at[way, t - 1], dev(dy=1 - 2 * way))

    def by_step(t):
        for way in (0, 1):
            arrived_at(by_landed(t, way), s_by.at[way, t - 1], r_by.at[way, t - 1])
        if t < 4:
            by_send(t + 1)
            bx_send(2 * t - 1)
            bx_send(2 * t)
        else:
            bx_send(7)

    def ay_piece(t, way):
        ref = wa.at[(y + (1 - t if way == 0 else t - 1) + 8) % 8]
        return ref if t < 4 else ref.at[pl.ds(way * 2, 2)]

    def ay_landed(t, way):
        ref = wa.at[(y + (-t if way == 0 else t) + 8) % 8]
        return ref if t < 4 else ref.at[pl.ds(way * 2, 2)]

    def ay_send(t):
        for way in (0, 1):
            piece = ay_piece(t, way)
            send(piece, piece, s_ay.at[way, t - 1], r_ay.at[way, t - 1], dev(dy=1 - 2 * way))

    def ax_done():
        for d in (1, 2, 3):
            arrived_at(wa.at[y, (x - d + 4) % 4], s_ax.at[d - 1], r_ax.at[d - 1])
        ay_send(1)

    def ay_step(t):
        for way in (0, 1):
            arrived_at(ay_landed(t, way), s_ay.at[way, t - 1], r_ay.at[way, t - 1])
        if t < 4:
            ay_send(t + 1)

    def bx_row(j):
        return (y + offset_of(j) + 8) % 8

    def bx_send(j):
        piece = wb.at[x, bx_row(j)]
        for way in (0, 1):
            send(piece, piece, s_bx.at[way, j], r_bx.at[way, j], dev(dx=1 - 2 * way))

    def bx_step(j):
        for way in (0, 1):
            landed = wb.at[(x + 2 * way - 1 + 4) % 4, bx_row(j)]
            arrived_at(landed, s_bx.at[way, j], r_bx.at[way, j])
        way = j % 2
        piece = wb.at[(x + 2 * way - 1 + 4) % 4, bx_row(j)]
        send(piece, piece, s_bx2.at[j], r_bx2.at[j], dev(dx=1 - 2 * way))

    def bx_last(j):
        arrived_at(wb.at[(x + 2) % 4, bx_row(j)], s_bx2.at[j], r_bx2.at[j])

    def halo():
        arrived_at(prevmeta, s_halo.at[1], r_halo.at[1])
        arrived_at(feat.at[:, pl.ds(0, 16)], s_halo.at[0], r_halo.at[0])
        prev_row = jnp.where(ctx == 0, -1.0, prevmeta[3:4, 0:128])
        mask = same_segment(prev_row)
        mask_s[...] = mask
        count = jnp.sum(mask[0:32], axis=1, keepdims=True)[0:16]
        one = jnp.where(count > 1.5, 1.0, 0.0)
        two = jnp.where(count > 2.5, 1.0, 0.0)
        pad = jnp.zeros((16, 1), F32)
        one = jnp.concatenate([pad, one], axis=0)
        two = jnp.concatenate([pad, two], axis=0)
        fixed = [
            featurize(i, feat[i, pl.ds(0, 32)].astype(F32), one, two)[16:32] for i in range(3)
        ]
        qf[pl.ds(0, 16), :] = fixed[0]
        win[pl.ds(128, 16), :] = (fixed[1] * fixed[2]).astype(BF)
        arrived_at(win.at[pl.ds(0, 128)], s_halo.at[2], r_halo.at[2])

    def conv(part):
        cols = pl.ds(pl.multiple_of(part * 256, 256), 256)
        window = win[:, cols]
        lane_group = iota((ROWS, 256), 1) // 16

        def step(i, total):
            stack = []
            for n in range(4):
                row = jnp.broadcast_to(hrev[pl.ds(part * 16 + i * 4 + n, 1), :], (TAPS, TAPS))
                turned = pltpu.roll(row, 0, 1, stride=1, stride_axis=0)
                tall = jnp.concatenate([turned, turned[0:32]], axis=0)
                wide = jnp.concatenate([tall, tall, tall], axis=1)
                stack.append(jnp.where(mask_s[...] > 0.5, wide, 0.0).astype(BF))
            res = jnp.dot(jnp.concatenate(stack, axis=0), window, preferred_element_type=F32)
            for n in range(4):
                total = jnp.where(
                    lane_group == i * 4 + n, res[n * ROWS:(n + 1) * ROWS], total
                )
            return total

        total = lax.fori_loop(0, 4, step, jnp.zeros((ROWS, 256), F32))
        center = win[pl.ds(128, ROWS), cols].astype(F32)
        return (qf[:, cols] * (total + gain[:, cols] * center)).astype(BF)

    def conv_theirs():
        gsend[...] = conv(kk)
        send(gsend, gbuf.at[mine_rows], s_gx.at[0], r_gx.at[0], sibling)

    def conv_mine():
        gbuf[mine_rows, :] = conv(k)

    def unit_cols(u):
        return pl.ds(u * 128, 128)

    def pack(u):
        if u == 0:
            other_rows = pl.ds(pl.multiple_of(kk * ROWS, 16), ROWS)
            arrived_at(slots.at[kk], s_gx.at[1], r_gx.at[1])
            arrived_at(cbuf.at[other_rows], s_gx.at[2], r_gx.at[2])
            arrived_at(gbuf.at[other_rows], s_gx.at[0], r_gx.at[0])
        slot = jnp.concatenate([slots[0, 0:1, 0:ROWS], slots[1, 0:1, 0:ROWS]], axis=1)
        place_row = iota((1024, 2 * ROWS), 0).astype(F32)
        pick = jnp.where(place_row == slot, 1.0, 0.0).astype(BF)
        res = jnp.dot(pick, gbuf[:, unit_cols(u)], preferred_element_type=F32)
        if u == 0:
            cslot = jnp.concatenate([slots[0, 1:2, 0:ROWS], slots[1, 1:2, 0:ROWS]], axis=1)
            cpick = jnp.where(place_row == cslot, 1.0, 0.0).astype(BF)
            res = res + jnp.dot(cpick, cbuf[...], preferred_element_type=F32)
        packed[u] = res.astype(BF)

        block = pl.ds(pl.multiple_of(chip * 32, 32), 32)
        pltpu.make_async_copy(packed.at[u, block], arrived.at[u, block], s_self.at[u]).start()

        def post(i, carry):
            dx = i % 4
            dy = offset_of(i // 4)
            other = ((x + dx) % 4) * 8 + (y + dy + 8) % 8
            theirs = pl.ds(pl.multiple_of(other * 32, 32), 32)
            pltpu.make_async_remote_copy(
                src_ref=packed.at[u, theirs], dst_ref=arrived.at[u, block],
                send_sem=s_rel.at[u], recv_sem=r_rel.at[u],
                device_id=(other * 2 + k, z), device_id_type=MESH,
            ).start()
            return carry

        lax.fori_loop(1, 32, post, 0)

    def relay_wait(u):
        block = pl.ds(pl.multiple_of(chip * 32, 32), 32)
        bulk = pltpu.make_async_remote_copy(
            src_ref=packed.at[u, pl.ds(0, 992)], dst_ref=arrived.at[u, pl.ds(0, 992)],
            send_sem=s_rel.at[u], recv_sem=r_rel.at[u],
            device_id=sibling, device_id_type=MESH,
        )
        bulk.wait_send()
        bulk.wait_recv()
        pltpu.make_async_copy(packed.at[u, block], arrived.at[u, block], s_self.at[u]).wait()

    def unpack(u):
        relay_wait(u)
        if u == 0:
            pickc = jnp.where(iota((32, 1024), 1) == iota((32, 1024), 0) * 32 + 20, 1.0, 0.0)
            costs = jnp.dot(pickc.astype(BF), arrived[0], preferred_element_type=F32)
            live = jnp.where(costs > 0.5, 1.0, 0.0)
            lane = iota((32, 128), 1)
            own = (lane >= k * 10) & (lane < k * 10 + 10)
            total = jnp.sum(jnp.where(own, costs, 0.0)) / (32.0 * ROWS)
            cost_out[...] = jnp.broadcast_to(total, (8, 128))
            a = iota((128, 128), 0)
            b = iota((128, 128), 1)
            both = (a // 10 == b // 10) & (a % 5 == 0) & (b < 20)
            first = both & (a % 10 == 0) & (b % 10 >= 5)
            live_b = live.astype(BF)
            tally = jnp.dot(live_b, jnp.where(both, 1.0, 0.0).astype(BF), preferred_element_type=F32)
            before = jnp.dot(live_b, jnp.where(first, 1.0, 0.0).astype(BF), preferred_element_type=F32)
            lower = jnp.where(iota((32, 32), 1) < iota((32, 32), 0), 1.0, 0.0)
            rank = jnp.dot(lower.astype(BF), tally.astype(BF), preferred_element_type=F32) + before
            code = jnp.where(live > 0.5, rank + 1.0, 0.0)
            spread = jnp.where(iota((128, 1024), 0) == iota((128, 1024), 1) % 32, 1.0, 0.0)
            wide = jnp.dot(code.astype(BF), spread.astype(BF), preferred_element_type=F32)
            mine_only = iota((32, 1024), 0) == iota((32, 1024), 1) // 32
            code_row = jnp.sum(jnp.where(mine_only, wide, 0.0), axis=0, keepdims=True)
            i_row = iota((1, 1024), 1) % 32
            core_row = i_row // 10
            dest = (core_row * ROWS + i_row % 5).astype(F32) + 5.0 * (code_row - 1.0)
            dest = jnp.where((code_row > 0.5) & (i_row < 20), dest, -1.0)
            hit = iota((2 * ROWS, 1024), 0).astype(F32) == dest
            dmat[...] = jnp.where(hit, 1.0, 0.0).astype(BF)
        rows = jnp.dot(dmat[...], arrived[u], preferred_element_type=F32).astype(BF)
        abuf[z * 2 + k, :, unit_cols(u)] = rows
        z_send(u, 1)
        mine_slot = abuf.at[z * 2 + k, :, unit_cols(u)]
        send(mine_slot, mine_slot, s_c.at[u, 0], r_c.at[u, 0], sibling)

    def z_slot(u, off, core):
        return abuf.at[((z + off + 8) % 8) * 2 + core, :, unit_cols(u)]

    def z_part(ref, t, way):
        return ref if t < 4 else ref.at[pl.ds(way * ROWS, ROWS)]

    def z_send(u, t):
        for way in (0, 1):
            piece = z_part(z_slot(u, 1 - t if way == 0 else t - 1, k), t, way)
            send(piece, piece, s_z.at[u, way, t - 1], r_z.at[u, way, t - 1], dev(dz=1 - 2 * way))

    def z_step(u, t):
        for way in (0, 1):
            landed = z_part(z_slot(u, -t if way == 0 else t, k), t, way)
            arrived_at(landed, s_z.at[u, way, t - 1], r_z.at[u, way, t - 1])
        if t < 4:
            z_send(u, t + 1)
        for j in ((2 * t - 1, 2 * t) if t < 4 else (7,)):
            piece = z_slot(u, offset_of(j), k)
            send(piece, piece, s_c.at[u, j], r_c.at[u, j], sibling)

    def multiply(first, last):
        def step(j, carry):
            zo = (z + offset_of(j) + 8) % 8
            for u in range(UNITS):
                arrived_at(abuf.at[zo * 2 + kk, :, unit_cols(u)], s_c.at[u, j], r_c.at[u, j])
            xs = zo // 2
            for half in (0, 1):
                ys = (zo % 2) * 4 + 2 * half
                part_a = jnp.concatenate([wa[ys, xs], wa[ys + 1, xs]], axis=0)
                part_b = jnp.concatenate([wb[xs, ys], wb[xs, ys + 1]], axis=0)
                weights = jnp.concatenate([part_a, part_b], axis=1)
                acc[...] += jnp.dot(
                    abuf[zo * 2 + half], weights, preferred_element_type=F32
                )
            return carry

        lax.fori_loop(first, last, step, 0)

    def clear():
        acc[...] = jnp.zeros_like(acc)

    def finish():
        theirs = pl.ds(pl.multiple_of(kk * ROWS, 16), ROWS)
        osend[...] = acc[theirs, :].astype(BF)
        send(osend, orecv, s_o, r_o, sibling)
        out[:, pl.ds(pl.multiple_of(k * 512, 512), 512)] = acc[mine_rows, :].astype(BF)
        arrived_at(orecv, s_o, r_o)
        out[:, pl.ds(pl.multiple_of(kk * 512, 512), 512)] = orecv[...]

    at(1.5, w_own)
    at(2.5, halo)
    at(2.6, conv_theirs)
    at(4.0, ax_done)
    at(5.1, conv_mine)
    for t, when in ((1, 5.0), (2, 8.6), (3, 11.0), (4, 13.0)):
        at(when, by_step, t)
    for t, when in ((1, 8.7), (2, 12.0), (3, 16.0), (4, 18.0)):
        at(when, ay_step, t)
    for j in range(8):
        at(5.0 + 2.9 * j, bx_step, j)
        at(8.5 + 2.9 * j, bx_last, j)
    at(8.0, pack, 0)
    at(8.5, pack, 1)
    at(9.0, clear)
    at(15.0, unpack, 0)
    at(20.0, unpack, 1)
    for t in (1, 2, 3, 4):
        at(15.0 + 2.8 * t, z_step, 0, t)
        at(21.0 + 2.8 * t, z_step, 1, t)
    at(31.0, multiply, 0, 7)
    at(33.0, multiply, 7, 8)
    at(40.0, finish)
    for _, _, run in sorted(events, key=lambda e: e[:2]):
        run()
    for c in pending:
        c.wait_send()


def local(features, segment_ids, feat_taps, mixer_filter, skip_gain, out_weight, targets, row_costs):
    parts = jnp.transpose(features, (1, 0, 2))
    seg = segment_ids.astype(F32)
    tgt = targets.astype(F32)
    cost = row_costs.astype(F32)
    pad = (0, 96)
    meta = jnp.stack(
        [
            jnp.pad(seg, pad, constant_values=-7.0),
            jnp.pad(tgt, pad, constant_values=-7.0),
            jnp.pad(cost, pad),
            jnp.pad(seg[32:], (0, 128)),
        ]
        + [jnp.zeros((256,), F32)] * 4
    )
    metac = jnp.stack([seg, tgt, cost], axis=1)
    vmem = pl.BlockSpec(memory_space=pltpu.VMEM)
    hbm = pl.BlockSpec(memory_space=pl.ANY)
    dma = pltpu.SemaphoreType.DMA
    u = UNITS
    flops = 2 * 320 * 4096 * 512
    out, cost_out = pl.pallas_call(
        mixer_kernel,
        out_shape=(
            jax.ShapeDtypeStruct((ROWS, 1024), BF),
            jax.ShapeDtypeStruct((8, 128), F32),
        ),
        in_specs=[hbm, hbm] + [vmem] * 5,
        out_specs=(vmem, vmem),
        scratch_shapes=[
            pltpu.VMEM((3, 16 + ROWS, 512), BF),
            pltpu.VMEM((ROWS, 512), F32),
            pltpu.VMEM((384, 512), BF),
            pltpu.VMEM((32, 128), F32),
            pltpu.VMEM((ROWS, 384), F32),
            pltpu.VMEM((ROWS, 256), BF),
            pltpu.VMEM((2 * ROWS, 256), BF),
            pltpu.VMEM((2 * ROWS, 128), BF),
            pltpu.VMEM((2, 8, 256), F32),
            pltpu.VMEM((8, 256), F32),
            pltpu.VMEM((u, 1024, 128), BF),
            pltpu.VMEM((u, 1024, 128), BF),
            pltpu.VMEM((2 * ROWS, 1024), BF),
            pltpu.VMEM((16, 2 * ROWS, 256), BF),
            pltpu.VMEM((8, 4, 128, ACOLS), BF),
            pltpu.VMEM((4, 8, 128, BCOLS), BF),
            pltpu.VMEM((2 * ROWS, 512), F32),
            pltpu.VMEM((ROWS, 512), BF),
            pltpu.VMEM((ROWS, 512), BF),
            dma, dma((2,)), dma((2,)), dma((2,)), dma((3,)), dma((3,)), dma((3,)), dma((3,)),
            dma((u,)), dma((u,)), dma((u,)),
            dma((3,)), dma((3,)), dma((2, 4)), dma((2, 4)), dma((2, 4)), dma((2, 4)),
            dma((2, 8)), dma((2, 8)), dma((8,)), dma((8,)),
            dma((u, 2, 4)), dma((u, 2, 4)), dma((u, 8)), dma((u, 8)), dma, dma,
        ],
        compiler_params=pltpu.CompilerParams(
            collective_id=0, has_side_effects=True, vmem_limit_bytes=48 * 2**20
        ),
        cost_estimate=pl.CostEstimate(flops=flops, bytes_accessed=16 * 2**20, transcendentals=0),
        name="mixer",
    )(parts, out_weight, feat_taps, mixer_filter, skip_gain[None, :], meta, metac)
    return out, cost_out[0, 0:1]


def solution(mesh):
    placed = (
        P("ctx", None, "ch"),
        P("ctx"),
        P(None, None, "ch"),
        P("ch", None),
        P("ch"),
        P("ctx", "ch"),
        P("ctx"),
        P("ctx"),
    )
    return jax.shard_map(
        local, mesh=mesh, in_specs=placed, out_specs=(P("ctx", "ch"), P("ctx")), check_vma=False
    )
```

time: 304 us -> 87.5 us (0.29)
  waiting for transfers between devices: 111 us -> 0 us
  other arithmetic: 90.5 us -> 2.09 us
  Pallas kernels: 0 us -> 79.9 us
  starting transfers between devices: 38.9 us -> 0 us
  local copies, waits for them, and re-layouts: 37.5 us -> 4.5 us
  between operations: 16.4 us -> 0.7 us
  matrix products: 7.53 us -> 0 us
    all_gather x2 -> x0, waiting for transfers between devices: 107 us -> none  [the longest x1 94.1 us: project(): lax.all_gather(out_weight, 'ctx', axis=0, tiled=True)]
    gather x63 -> x0, other arithmetic: 82.1 us -> none  [the longest x59 42 us: relay_rows(): is_live = within < arrived_counts[sender]]
    pallas_call x0 -> x1, Pallas kernels: none -> 79.9 us  [local(): pl.pallas_call(mixer_kernel, out_shape=(jax.ShapeDtypeStruct((ROWS, 1024)...]
    all_to_all x3 -> x0, starting transfers between devices: 26.9 us -> none  [the longest x1 11.7 us: relay_rows(): lax.all_to_all(counts, 'ctx', split_axis=0, concat_axis=0, tiled=True)]
    gather x14 -> x0, local copies, waits for them, and re-layouts: 26.5 us -> none  [the longest x2 16.1 us: local(): jnp.take(filter_half, jnp.clip(lag_table, 0, tap_count - 1), axis=1)]
    ppermute x4 -> x0, starting transfers between devices: 12 us -> none  [passed_along(): return lax.ppermute(x, axis, pairs)]
    dot_general x6 -> x0, matrix products: 7.53 us -> none  [the longest x1 5.56 us: project(): jnp.dot(all_channels, lax.all_gather(out_weight, 'ctx', axis=0, tiled=Tru...]
    scatter x3 -> x0, local copies, waits for them, and re-layouts: 4.19 us -> none  [the longest x1 1.96 us: relay_rows(): placed = jnp.zeros((row_count + 1, row_block.shape[1]), row_block.dtype)....]
  transfers between devices with their start and end apart: 9 -> 0, of which waited for: 4 -> 0; matrix products, arithmetic and copies ran while one was open for 42% -> 0% of each run, Pallas kernels for 0% -> 0%
where the time goes in v1:
time: 87.5 us; the launch traced here: 87.2 us
  Pallas kernels  79.9 us (91%)
  local copies, waits for them, and re-layouts  4.5 us (5%)
  other arithmetic  2.09 us (2%)
    pallas_call x1, Pallas kernels, local(): pl.pallas_call(mixer_kernel, out_shape=(jax.ShapeDtypeStruct((ROWS, 1024)...  79.9 us
    unnamed x11, local copies, waits for them, and re-layouts  3.76 us

profile of v1, /device:TPU:1, one launch (start us, length us, event | category | flops | bytes accessed | tf_op | source)
XLA Modules:
  0.0 87.2 jit_solution(5777100283839845065)
XLA Ops:
  0.6 0.0 copy-start.1
  0.6 0.7 convert_element_type.13
  1.4 0.1 slice.6
  1.4 0.7 convert_element_type.14
  2.1 0.7 convert_element_type.15
  2.9 0.0 copy-start.3
  2.9 0.1 copy.13.metac
  3.0 0.0 copy-done.1
  3.0 0.6 copy-done.3
  3.6 0.0 copy-start
  3.6 1.0 %copy-done = bf16[160,3,512]{2,0,1:T(8,128)(2,1)S(1)} copy-done((bf16[160,3,512]{2,0,1:T(8,128)(2,1)S(1)}, bf16[160,3,512]{2,0,1:T(8,128)(2,1)}, u32[]{:S(2)}) %copy-start) | copy-done | bytes 491544
  4.6 0.0 copy-start.2
  4.6 0.7 copy-done.2
  5.4 0.0 copy-start.4
  5.4 0.7 copy-done.4
  6.0 79.9 %mixer.1 = (bf16[160,1024]{1,0:T(8,128)(2,1)S(1)}, f32[8,128]{1,0:T(8,128)S(1)}) custom-call(bf16[3,160,512]{2,1,0:T(8,128)(2,1)S(1)} %bitcast.10, bf16[64,1024]{1,0:T(8,128)(2,1)S(1)} %copy-done.1, f32[3,3,512]{2,1,0:T(4,128)S(1)} %copy-done.2, f32[32,128]{1,0:T(8,128)S(1)} %copy-done.3, f32[1,512]{1,0:T(1,128)S(1)} %bitcast.11, f32[8,256]{1,0:T(8,128)S(1)} %stack.35.meta, ...), custom_call_target="tpu_custom_call" | custom-call | flops 1342177280 | bytes 16777216 | tf_op jit(solution)/shard_map/mixer/pallas_call | solution.py:474
  85.9 0.5 slice.7
  86.4 0.7 copy.15
  (7 shorter events, 0.1 us)
Async XLA Ops:
  0.6 2.4 %copy-start.1 = (bf16[64,1024]{1,0:T(8,128)(2,1)S(1)}, bf16[64,1024]{1,0:T(8,128)(2,1)}, u32[]{:S(2)}) copy-start(bf16[64,1024]{1,0:T(8,128)(2,1)} %w_in.1) | copy-start | bytes 393220
  2.9 0.7 copy-start.3
  3.6 1.0 %copy-start = (bf16[160,3,512]{2,0,1:T(8,128)(2,1)S(1)}, bf16[160,3,512]{2,0,1:T(8,128)(2,1)}, u32[]{:S(2)}) copy-start(bf16[160,3,512]{2,0,1:T(8,128)(2,1)} %param.8) | copy-start | bytes 1474564
  4.6 0.7 copy-start.2
  5.4 0.7 copy-start.4

commit v2 on v1

v2 whole, which is shorter than its diff:
```python
import functools

import jax
import jax.numpy as jnp
from jax import lax
from jax.experimental import pallas as pl
from jax.experimental.pallas import tpu as pltpu
from jax.sharding import PartitionSpec as P

MESH = pl.DeviceIdType.MESH
BF = jnp.bfloat16
F32 = jnp.float32
ROWS = 160
TAPS = 128
UNITS = 2
ACOLS = 128
BCOLS = 384


def place():
    ctx = lax.axis_index("ctx")
    return ctx // 16, (ctx // 2) % 8, ctx % 2, lax.axis_index("ch"), ctx


def offset_of(j):
    return ((j + 1) // 2) * (2 * (j % 2) - 1)


def iota(shape, dim):
    return lax.broadcasted_iota(jnp.int32, shape, dim)


def mixer_kernel(
    feat_in, w_in, taps_in, filt_in, gain_in, seg_in, tgt_in, cost_in,
    out, cost_out,
    taps, filt, gain, seg_v, tgt_v, cost_v, meta, s_in, feat, qf, win, hrev, circ, mask_a, mask_b, gsend, gbuf, cbuf, slots, prevmeta,
    packed, arrived, abuf, wa, wb, acc, osend, orecv,
    s_feat, s_loc, s_sib, r_sib, s_halo, r_halo, s_gx, r_gx, s_rel, r_rel, s_self,
    s_ax, r_ax, s_ay, r_ay, s_by, r_by, s_bx, r_bx, s_bx2, r_bx2,
    s_z, r_z, s_c, r_c, s_o, r_o,
):
    x, y, k, z, ctx = place()
    chip = x * 8 + y
    kk = 1 - k

    def dev(dx=0, dy=0, dz=0, dk=0):
        return (
            (((x + dx + 4) % 4) * 8 + (y + dy + 8) % 8) * 2 + (k + dk) % 2,
            (z + dz + 8) % 8,
        )

    sibling = dev(dk=1)
    following = ((ctx + 1) % 64, z)
    previous = ((ctx + 63) % 64, z)
    pending = []

    def send(src, dst, ssem, rsem, to):
        c = pltpu.make_async_remote_copy(
            src_ref=src, dst_ref=dst, send_sem=ssem, recv_sem=rsem,
            device_id=to, device_id_type=MESH,
        )
        c.start()
        pending.append(c)

    def arrived_at(dst, ssem, rsem):
        pltpu.make_async_remote_copy(
            src_ref=dst, dst_ref=dst, send_sem=ssem, recv_sem=rsem,
            device_id=sibling, device_id_type=MESH,
        ).wait_recv()

    own_a = wa.at[y, x]
    own_b = wb.at[x, y]
    mine = pl.ds(pl.multiple_of(k * 64, 64), 64)

    def wcols(core, first, count):
        return w_in.at[:, pl.ds(pl.multiple_of(core * 512 + first, 128), count)]

    def start_weights():
        copies = (
            pltpu.make_async_copy(wcols(k, 0, ACOLS), own_a.at[mine], s_loc.at[0]),
            pltpu.make_async_copy(wcols(k, ACOLS, BCOLS), own_b.at[mine], s_loc.at[1]),
        )
        for c in copies:
            c.start()
        return copies

    load = pltpu.make_async_copy(feat_in, feat.at[:, pl.ds(16, ROWS)], s_feat)
    load.start()
    w_loads = start_weights()
    loads = [
        pltpu.make_async_copy(src, dst, s_in.at[n])
        for n, (src, dst) in enumerate(
            ((seg_in, seg_v), (tgt_in, tgt_v), (cost_in, cost_v),
             (taps_in, taps), (filt_in, filt), (gain_in, gain))
        )
    ]
    for c in loads:
        c.start()
    barrier = pltpu.get_barrier_semaphore()

    def greet(i, carry):
        other = (chip + i) % 32
        pl.semaphore_signal(barrier, inc=1, device_id=(other * 2 + k, z), device_id_type=MESH)
        return carry

    lax.fori_loop(1, 32, greet, 0)
    for to in (sibling, following, previous, dev(dz=1), dev(dz=-1)):
        pl.semaphore_signal(barrier, inc=1, device_id=to, device_id_type=MESH)

    for c in loads:
        c.wait()

    def row_of(ref, fill):
        return jnp.concatenate([ref[...].astype(F32), jnp.full((1, 96), fill, F32)], axis=1)

    seg_pad = row_of(seg_v, -7.0)
    meta[0:1, :] = seg_pad
    meta[1:2, :] = row_of(tgt_v, -7.0)
    meta[2:3, :] = row_of(cost_v, 0.0)
    meta[3:4, :] = pltpu.roll(seg_pad, 256 - 32, 1)
    meta[4:8, :] = jnp.zeros((4, 256), F32)
    metac = meta[...].T[0:ROWS]
    seg_col = metac[:, 0:1]
    tgt_col = metac[:, 1:2]
    cost_col = metac[:, 2:3]
    lag = iota((ROWS, 384), 0) + TAPS - iota((ROWS, 384), 1)
    in_reach = (lag >= 0) & (lag < TAPS)

    def same_segment(prev_row):
        seg_row = jnp.concatenate([prev_row, meta[0:1, :]], axis=1)
        return jnp.where(in_reach & (seg_col == seg_row), 1.0, 0.0)

    def featurize(index, center, match_one, match_two):
        return (
            taps[index, 0:1, :] * center
            + taps[index, 1:2, :] * pltpu.roll(center, 1, 0) * match_one
            + taps[index, 2:3, :] * pltpu.roll(center, 2, 0) * match_two
        )

    seg_own = same_segment(jnp.full((1, 128), -1.0, F32))
    back = jnp.sum(seg_own, axis=1, keepdims=True)
    m_one = jnp.where(back > 1.5, 1.0, 0.0)
    m_two = jnp.where(back > 2.5, 1.0, 0.0)
    load.wait()
    own_rows = pl.ds(16, ROWS)
    qf[...] = featurize(0, feat[0, own_rows].astype(F32), m_one, m_two)
    win[pl.ds(128, ROWS), :] = (
        featurize(1, feat[1, own_rows].astype(F32), m_one, m_two)
        * featurize(2, feat[2, own_rows].astype(F32), m_one, m_two)
    ).astype(BF)
    win[pl.ds(288, 96), :] = jnp.zeros((96, 512), BF)

    pl.semaphore_wait(barrier, 36)

    send(wcols(kk, 0, ACOLS), own_a.at[mine], s_sib.at[0], r_sib.at[0], sibling)
    send(wcols(kk, ACOLS, BCOLS), own_b.at[mine], s_sib.at[1], r_sib.at[1], sibling)
    send(feat.at[:, pl.ds(160, 16)], feat.at[:, pl.ds(0, 16)], s_halo.at[0], r_halo.at[0], following)
    send(meta, prevmeta, s_halo.at[1], r_halo.at[1], following)
    send(win.at[pl.ds(160, 128)], win.at[pl.ds(0, 128)], s_halo.at[2], r_halo.at[2], following)
    tgt_row = meta[1:2, :]
    same_target = tgt_col == tgt_row
    rq = iota((ROWS, 256), 0)
    rr = iota((ROWS, 256), 1)
    rank_row = jnp.sum(jnp.where(same_target & (rq < rr), 1.0, 0.0), axis=0, keepdims=True)
    rank_col = jnp.sum(jnp.where(same_target & (rr < rq), 1.0, 0.0), axis=1, keepdims=True)
    kf = k.astype(F32)
    mine_rows = pl.ds(pl.multiple_of(k * ROWS, 16), ROWS)
    chip_row = jnp.floor(tgt_row * 0.5)
    core_row = tgt_row - 2.0 * chip_row
    for u in range(UNITS):
        here = core_row == u
        slots[k, 2 * u:2 * u + 1, :] = jnp.where(here, chip_row * 16.0 + kf * 5.0 + rank_row, -1.0)
        slots[k, 2 * u + 1:2 * u + 2, :] = jnp.where(here, chip_row * 16.0 + 10.0, -1.0)
    slots[k, 4:8, :] = jnp.zeros((4, 256), F32)
    cbuf[mine_rows, :] = jnp.where(
        iota((ROWS, 128), 1).astype(F32) == kf * 5.0 + rank_col, cost_col, 0.0
    ).astype(BF)

    flip = (iota((TAPS, TAPS), 0) + iota((TAPS, TAPS), 1)) % TAPS == 0
    hrev[...] = jnp.dot(
        filt[...].astype(BF), jnp.where(flip, 1.0, 0.0).astype(BF), preferred_element_type=F32
    )

    send(slots.at[k], slots.at[k], s_gx.at[1], r_gx.at[1], sibling)
    send(cbuf.at[mine_rows], cbuf.at[mine_rows], s_gx.at[2], r_gx.at[2], sibling)

    def turn(i, carry):
        for n in range(4):
            row = jnp.broadcast_to(hrev[pl.ds(i * 4 + n, 1), :], (TAPS, TAPS))
            circ[i * 4 + n] = pltpu.roll(row, 0, 1, stride=1, stride_axis=0).astype(BF)
        return carry

    lax.fori_loop(0, 8, turn, 0)

    events = []

    def at(when, what, *args):
        events.append((when, len(events), functools.partial(what, *args)))

    def w_own():
        theirs = pl.ds(pl.multiple_of(kk * 64, 64), 64)
        for c in w_loads:
            c.wait()
        arrived_at(own_a.at[theirs], s_sib.at[0], r_sib.at[0])
        arrived_at(own_b.at[theirs], s_sib.at[1], r_sib.at[1])
        for d in (1, 2, 3):
            send(own_a, own_a, s_ax.at[d - 1], r_ax.at[d - 1], dev(dx=d))
        by_send(1)
        bx_send(0)

    def by_piece(t, way):
        ref = wb.at[x, (y + (1 - t if way == 0 else t - 1) + 8) % 8]
        return ref if t < 4 else ref.at[pl.ds(way * 64, 64)]

    def by_landed(t, way):
        ref = wb.at[x, (y + (-t if way == 0 else t) + 8) % 8]
        return ref if t < 4 else ref.at[pl.ds(way * 64, 64)]

    def by_send(t):
        for way in (0, 1):
            piece = by_piece(t, way)
            send(piece, piece, s_by.at[way, t - 1], r_by.at[way, t - 1], dev(dy=1 - 2 * way))

    def by_step(t):
        for way in (0, 1):
            arrived_at(by_landed(t, way), s_by.at[way, t - 1], r_by.at[way, t - 1])
        if t < 4:
            bx_send(2 * t - 1)
            bx_send(2 * t)
        else:
            bx_send(7)

    def ay_piece(t, way):
        ref = wa.at[(y + (1 - t if way == 0 else t - 1) + 8) % 8]
        return ref if t < 4 else ref.at[pl.ds(way * 2, 2)]

    def ay_landed(t, way):
        ref = wa.at[(y + (-t if way == 0 else t) + 8) % 8]
        return ref if t < 4 else ref.at[pl.ds(way * 2, 2)]

    def ay_send(t):
        for way in (0, 1):
            piece = ay_piece(t, way)
            send(piece, piece, s_ay.at[way, t - 1], r_ay.at[way, t - 1], dev(dy=1 - 2 * way))

    def ax_done():
        for d in (1, 2, 3):
            arrived_at(wa.at[y, (x - d + 4) % 4], s_ax.at[d - 1], r_ax.at[d - 1])
        ay_send(1)

    def ay_step(t):
        for way in (0, 1):
            arrived_at(ay_landed(t, way), s_ay.at[way, t - 1], r_ay.at[way, t - 1])
        if t < 4:
            ay_send(t + 1)

    def bx_row(j):
        return (y + offset_of(j) + 8) % 8

    def bx_send(j):
        piece = wb.at[x, bx_row(j)]
        for way in (0, 1):
            send(piece, piece, s_bx.at[way, j], r_bx.at[way, j], dev(dx=1 - 2 * way))

    def bx_step(j):
        for way in (0, 1):
            landed = wb.at[(x + 2 * way - 1 + 4) % 4, bx_row(j)]
            arrived_at(landed, s_bx.at[way, j], r_bx.at[way, j])
        way = j % 2
        piece = wb.at[(x + 2 * way - 1 + 4) % 4, bx_row(j)]
        send(piece, piece, s_bx2.at[j], r_bx2.at[j], dev(dx=1 - 2 * way))

    def w_last():
        for j in range(8):
            arrived_at(wb.at[(x + 2) % 4, bx_row(j)], s_bx2.at[j], r_bx2.at[j])

    def halo():
        arrived_at(prevmeta, s_halo.at[1], r_halo.at[1])
        arrived_at(feat.at[:, pl.ds(0, 16)], s_halo.at[0], r_halo.at[0])
        prev_row = jnp.where(ctx == 0, -1.0, prevmeta[3:4, 0:128])
        mask = same_segment(prev_row)
        mask_a[...] = mask[0:128, 0:256].astype(BF)
        mask_b[...] = mask[128:160, 128:384].astype(BF)
        count = jnp.sum(mask[0:32], axis=1, keepdims=True)[0:16]
        one = jnp.where(count > 1.5, 1.0, 0.0)
        two = jnp.where(count > 2.5, 1.0, 0.0)
        pad = jnp.zeros((16, 1), F32)
        one = jnp.concatenate([pad, one], axis=0)
        two = jnp.concatenate([pad, two], axis=0)
        fixed = [
            featurize(i, feat[i, pl.ds(0, 32)].astype(F32), one, two)[16:32] for i in range(3)
        ]
        qf[pl.ds(0, 16), :] = fixed[0]
        win[pl.ds(128, 16), :] = (fixed[1] * fixed[2]).astype(BF)
        arrived_at(win.at[pl.ds(0, 128)], s_halo.at[2], r_halo.at[2])

    def conv(part, dst, dst_rows):
        lane_group = iota((TAPS, 128), 1) // 16
        for tile in range(2):
            cols = pl.ds(pl.multiple_of(part * 256 + tile * 128, 128), 128)
            tall, low = [], []
            for n in range(8):
                turned = circ[part * 16 + tile * 8 + n]
                pair = jnp.concatenate([turned, turned], axis=1)
                tall.append(pair * mask_a[...])
                low.append(pair[0:32] * mask_b[...])
            res_a = jnp.dot(
                jnp.concatenate(tall, axis=0), win[pl.ds(0, 256), cols], preferred_element_type=F32
            )
            res_b = jnp.dot(
                jnp.concatenate(low, axis=0), win[pl.ds(128, 256), cols], preferred_element_type=F32
            )
            top, bottom = res_a[0:128], res_b[0:32]
            for n in range(1, 8):
                top = jnp.where(lane_group == n, res_a[n * 128:(n + 1) * 128], top)
                bottom = jnp.where(lane_group[0:32] == n, res_b[n * 32:(n + 1) * 32], bottom)
            total = jnp.concatenate([top, bottom], axis=0)
            center = win[pl.ds(128, ROWS), cols].astype(F32)
            dst[dst_rows, pl.ds(tile * 128, 128)] = (
                qf[:, cols] * (total + gain[:, cols] * center)
            ).astype(BF)

    def conv_theirs():
        conv(kk, gsend, pl.ds(0, ROWS))
        send(gsend, gbuf.at[mine_rows], s_gx.at[0], r_gx.at[0], sibling)

    def conv_mine():
        conv(k, gbuf, mine_rows)

    totals = []

    def unit_rows(u):
        return pl.ds(u * ROWS, ROWS)

    def pack(u):
        if u == 0:
            other_rows = pl.ds(pl.multiple_of(kk * ROWS, 16), ROWS)
            arrived_at(slots.at[kk], s_gx.at[1], r_gx.at[1])
            arrived_at(cbuf.at[other_rows], s_gx.at[2], r_gx.at[2])
            arrived_at(gbuf.at[other_rows], s_gx.at[0], r_gx.at[0])

        def pick(n):
            slot = jnp.concatenate([slots[0, n:n + 1, 0:ROWS], slots[1, n:n + 1, 0:ROWS]], axis=1)
            return jnp.where(iota((512, 2 * ROWS), 0).astype(F32) == slot, 1.0, 0.0).astype(BF)

        res = jnp.dot(pick(2 * u), gbuf[...], preferred_element_type=F32)
        costs = jnp.dot(pick(2 * u + 1), cbuf[...], preferred_element_type=F32)
        res = jnp.concatenate([res[:, 0:128] + costs, res[:, 128:256]], axis=1)
        packed[u] = res.astype(BF)

        block = pl.ds(pl.multiple_of(chip * 16, 16), 16)
        pltpu.make_async_copy(packed.at[u, block], arrived.at[u, block], s_self.at[u]).start()

        def post(i, carry):
            dx = i % 4
            dy = offset_of(i // 4)
            other = ((x + dx) % 4) * 8 + (y + dy + 8) % 8
            theirs = pl.ds(pl.multiple_of(other * 16, 16), 16)
            pltpu.make_async_remote_copy(
                src_ref=packed.at[u, theirs], dst_ref=arrived.at[u, block],
                send_sem=s_rel.at[u], recv_sem=r_rel.at[u],
                device_id=(other * 2 + k, z), device_id_type=MESH,
            ).start()
            return carry

        lax.fori_loop(1, 32, post, 0)

    def relay_wait(u):
        block = pl.ds(pl.multiple_of(chip * 16, 16), 16)
        bulk = pltpu.make_async_remote_copy(
            src_ref=packed.at[u, pl.ds(0, 496)], dst_ref=arrived.at[u, pl.ds(0, 496)],
            send_sem=s_rel.at[u], recv_sem=r_rel.at[u],
            device_id=sibling, device_id_type=MESH,
        )
        bulk.wait_send()
        bulk.wait_recv()
        pltpu.make_async_copy(packed.at[u, block], arrived.at[u, block], s_self.at[u]).wait()

    def unpack(u):
        relay_wait(u)
        pickc = jnp.where(iota((32, 512), 1) == iota((32, 512), 0) * 16 + 10, 1.0, 0.0)
        costs = jnp.dot(pickc.astype(BF), arrived[u, :, 0:128], preferred_element_type=F32)
        totals.append(jnp.sum(costs) / (32.0 * ROWS))
        live = jnp.where(costs > 0.5, 1.0, 0.0)
        a = iota((128, 128), 0)
        b = iota((128, 128), 1)
        both = (a % 5 == 0) & (a < 10) & (b < 10)
        first = (a == 0) & (b >= 5) & (b < 10)
        live_b = live.astype(BF)
        tally = jnp.dot(live_b, jnp.where(both, 1.0, 0.0).astype(BF), preferred_element_type=F32)
        before = jnp.dot(live_b, jnp.where(first, 1.0, 0.0).astype(BF), preferred_element_type=F32)
        lower = jnp.where(iota((32, 32), 1) < iota((32, 32), 0), 1.0, 0.0)
        rank = jnp.dot(lower.astype(BF), tally.astype(BF), preferred_element_type=F32) + before
        code = jnp.where(live > 0.5, rank + 1.0, 0.0)
        spread = jnp.where(iota((128, 512), 0) == iota((128, 512), 1) % 16, 1.0, 0.0)
        wide = jnp.dot(code.astype(BF), spread.astype(BF), preferred_element_type=F32)
        mine_only = iota((32, 512), 0) == iota((32, 512), 1) // 16
        code_row = jnp.sum(jnp.where(mine_only, wide, 0.0), axis=0, keepdims=True)
        i_row = iota((1, 512), 1) % 16
        dest = (i_row % 5).astype(F32) + 5.0 * (code_row - 1.0)
        dest = jnp.where((code_row > 0.5) & (i_row < 10), dest, -1.0)
        hit = jnp.where(iota((ROWS, 512), 0).astype(F32) == dest, 1.0, 0.0).astype(BF)
        rows = jnp.dot(hit, arrived[u], preferred_element_type=F32).astype(BF)
        abuf[z * 2 + k, unit_rows(u), :] = rows
        z_send(u, 1)
        mine_slot = abuf.at[z * 2 + k, unit_rows(u)]
        send(mine_slot, mine_slot, s_c.at[u, 0], r_c.at[u, 0], sibling)

    def z_slot(u, off, core):
        return abuf.at[((z + off + 8) % 8) * 2 + core, unit_rows(u)]

    def z_part(ref, t, way):
        return ref if t < 4 else ref.at[pl.ds(way * 80, 80)]

    def z_send(u, t):
        for way in (0, 1):
            piece = z_part(z_slot(u, 1 - t if way == 0 else t - 1, k), t, way)
            send(piece, piece, s_z.at[u, way, t - 1], r_z.at[u, way, t - 1], dev(dz=1 - 2 * way))

    def z_step(u, t):
        for way in (0, 1):
            landed = z_part(z_slot(u, -t if way == 0 else t, k), t, way)
            arrived_at(landed, s_z.at[u, way, t - 1], r_z.at[u, way, t - 1])
        if t < 4:
            z_send(u, t + 1)
        for j in ((2 * t - 1, 2 * t) if t < 4 else (7,)):
            piece = z_slot(u, offset_of(j), k)
            send(piece, piece, s_c.at[u, j], r_c.at[u, j], sibling)

    def multiply(first, last):
        def step(j, carry):
            zo = (z + offset_of(j) + 8) % 8
            for u in range(UNITS):
                arrived_at(abuf.at[zo * 2 + kk, unit_rows(u)], s_c.at[u, j], r_c.at[u, j])
            xs = zo // 2
            for half in (0, 1):
                ys = (zo % 2) * 4 + 2 * half
                part_a = jnp.concatenate([wa[ys, xs], wa[ys + 1, xs]], axis=0)
                part_b = jnp.concatenate([wb[xs, ys], wb[xs, ys + 1]], axis=0)
                weights = jnp.concatenate([part_a, part_b], axis=1)
                acc[...] += jnp.dot(
                    abuf[zo * 2 + half], weights, preferred_element_type=F32
                )
            return carry

        lax.fori_loop(first, last, step, 0)

    def clear():
        acc[...] = jnp.zeros_like(acc)

    def finish():
        theirs = pl.ds(pl.multiple_of(kk * ROWS, 16), ROWS)
        cost_out[0] = jnp.where(k == 0, totals[0], totals[1])
        osend[...] = acc[theirs, :].astype(BF)
        send(osend, orecv, s_o, r_o, sibling)
        out[:, pl.ds(pl.multiple_of(k * 512, 512), 512)] = acc[mine_rows, :].astype(BF)
        arrived_at(orecv, s_o, r_o)
        out[:, pl.ds(pl.multiple_of(kk * 512, 512), 512)] = orecv[...]

    plan = (
        (w_own, 1),
        (halo, 2),
        (conv_theirs, 3),
        (ax_done, 4),
        (by_step, 5, 1),
        (by_send, 6, 2),
        (conv_mine, 7),
        (pack, 8, 0),
        (pack, 9, 1),
        (clear, 10),
        (bx_step, 11, 0),
        (by_step, 12, 2),
        (bx_step, 13, 1),
        (bx_step, 14, 2),
        (unpack, 15, 0),
        (by_send, 16, 3),
        (unpack, 17, 1),
        (ay_step, 18, 1),
        (z_step, 19, 0, 1),
        (by_step, 20, 3),
        (by_send, 21, 4),
        (bx_step, 22, 3),
        (bx_step, 23, 4),
        (z_step, 24, 1, 1),
        (ay_step, 25, 2),
        (z_step, 26, 0, 2),
        (by_step, 27, 4),
        (bx_step, 28, 5),
        (z_step, 29, 1, 2),
        (bx_step, 30, 6),
        (ay_step, 31, 3),
        (z_step, 32, 0, 3),
        (bx_step, 33, 7),
        (z_step, 34, 1, 3),
        (ay_step, 35, 4),
        (w_last, 36),
        (multiply, 37, 0, 5),
        (z_step, 38, 0, 4),
        (z_step, 39, 1, 4),
        (multiply, 40, 5, 8),
        (finish, 41),
    )
    for what, when, *args in plan:
        at(when, what, *args)
    for _, _, run in sorted(events, key=lambda e: e[:2]):
        run()
    for c in pending:
        c.wait_send()


def local(features, segment_ids, feat_taps, mixer_filter, skip_gain, out_weight, targets, row_costs):
    parts = jnp.transpose(features, (1, 0, 2))
    vmem = pl.BlockSpec(memory_space=pltpu.VMEM)
    hbm = pl.BlockSpec(memory_space=pltpu.HBM)
    dma = pltpu.SemaphoreType.DMA
    u = UNITS
    flops = 2 * 320 * 4096 * 512
    out, cost_out = pl.pallas_call(
        mixer_kernel,
        out_shape=(
            jax.ShapeDtypeStruct((ROWS, 1024), BF),
            jax.ShapeDtypeStruct((1,), F32),
        ),
        in_specs=[hbm] * 8,
        out_specs=(vmem, pl.BlockSpec(memory_space=pltpu.SMEM)),
        scratch_shapes=[
            pltpu.VMEM((3, 3, 512), F32),
            pltpu.VMEM((32, TAPS), F32),
            pltpu.VMEM((1, 512), F32),
            pltpu.VMEM((1, ROWS), jnp.int32),
            pltpu.VMEM((1, ROWS), jnp.int32),
            pltpu.VMEM((1, ROWS), jnp.int32),
            pltpu.VMEM((8, 256), F32),
            dma((6,)),
            pltpu.VMEM((3, 16 + ROWS, 512), BF),
            pltpu.VMEM((ROWS, 512), F32),
            pltpu.VMEM((384, 512), BF),
            pltpu.VMEM((32, 128), F32),
            pltpu.VMEM((32, TAPS, TAPS), BF),
            pltpu.VMEM((128, 256), BF),
            pltpu.VMEM((32, 256), BF),
            pltpu.VMEM((ROWS, 256), BF),
            pltpu.VMEM((2 * ROWS, 256), BF),
            pltpu.VMEM((2 * ROWS, 128), BF),
            pltpu.VMEM((2, 8, 256), F32),
            pltpu.VMEM((8, 256), F32),
            pltpu.VMEM((u, 512, 256), BF),
            pltpu.VMEM((u, 512, 256), BF),
            pltpu.VMEM((16, 2 * ROWS, 256), BF),
            pltpu.VMEM((8, 4, 128, ACOLS), BF),
            pltpu.VMEM((4, 8, 128, BCOLS), BF),
            pltpu.VMEM((2 * ROWS, 512), F32),
            pltpu.VMEM((ROWS, 512), BF),
            pltpu.VMEM((ROWS, 512), BF),
            dma, dma((2,)), dma((2,)), dma((2,)), dma((3,)), dma((3,)), dma((3,)), dma((3,)),
            dma((u,)), dma((u,)), dma((u,)),
            dma((3,)), dma((3,)), dma((2, 4)), dma((2, 4)), dma((2, 4)), dma((2, 4)),
            dma((2, 8)), dma((2, 8)), dma((8,)), dma((8,)),
            dma((u, 2, 4)), dma((u, 2, 4)), dma((u, 8)), dma((u, 8)), dma, dma,
        ],
        compiler_params=pltpu.CompilerParams(
            collective_id=0, has_side_effects=True, vmem_limit_bytes=60 * 2**20
        ),
        cost_estimate=pl.CostEstimate(flops=flops, bytes_accessed=16 * 2**20, transcendentals=0),
        name="mixer",
    )(
        parts, out_weight, feat_taps, mixer_filter, skip_gain[None, :],
        segment_ids[None, :], targets[None, :], row_costs[None, :],
    )
    return out, cost_out


def solution(mesh):
    placed = (
        P("ctx", None, "ch"),
        P("ctx"),
        P(None, None, "ch"),
        P("ch", None),
        P("ch"),
        P("ctx", "ch"),
        P("ctx"),
        P("ctx"),
    )
    return jax.shard_map(
        local, mesh=mesh, in_specs=placed, out_specs=(P("ctx", "ch"), P("ctx")), check_vma=False
    )
```

time: 87.5 us -> 68.8 us (0.79)
  Pallas kernels: 79.9 us -> 64.5 us
  local copies, waits for them, and re-layouts: 4.5 us -> 1.72 us
  other arithmetic: 2.09 us -> 0 us
  between operations: 0.7 us -> 2.33 us
    pallas_call x1, Pallas kernels: 79.9 us -> 64.5 us  [local(): pl.pallas_call(mixer_kernel, out_shape=(jax.ShapeDtypeStruct((ROWS, 1024)...]
    convert_element_type x3 -> x0, other arithmetic: 2.08 us -> none  [the longest x1 0.72 us: local(): seg = segment_ids.astype(F32)]
    unnamed x11 -> x1, local copies, waits for them, and re-layouts: 3.76 us -> 1.72 us
where the time goes in v2:
time: 68.8 us; the launch traced here: 68.6 us
  Pallas kernels  64.5 us (94%)
  between operations  2.33 us (3%)
  local copies, waits for them, and re-layouts  1.72 us (2%)
    pallas_call x1, Pallas kernels, local(): pl.pallas_call(mixer_kernel, out_shape=(jax.ShapeDtypeStruct((ROWS, 1024)...  64.5 us
    unnamed x1, local copies, waits for them, and re-layouts  1.72 us

profile of v2, /device:TPU:1, one launch (start us, length us, event | category | flops | bytes accessed | tf_op | source)
XLA Modules:
  0.0 68.6 jit_solution(3187220180588275357)
XLA Ops:
  0.6 64.5 %mixer.1 = (bf16[160,1024]{1,0:T(8,128)(2,1)}, f32[1]{0:T(128)}) custom-call(bf16[3,160,512]{2,1,0:T(8,128)(2,1)} %bitcast.5, bf16[64,1024]{1,0:T(8,128)(2,1)} %w_in.1, f32[3,3,512]{2,1,0:T(4,128)} %taps_in.1, f32[32,128]{1,0:T(8,128)} %filt_in.1, f32[1,512]{1,0:T(1,128)} %bitcast.6, s32[1,160]{1,0:T(1,128)} %bitcast.7, s32[1,160]{1,0:T(1,128)} %bitcast.8, ...), custom_call_target="tpu_custom_call" | custom-call | flops 1342177280 | bytes 16777216 | tf_op jit(solution)/shard_map/mixer/pallas_call | solution.py:518
  65.2 1.7 %copy.12 = bf16[160,1024]{1,0:T(8,128)(2,1)} copy(bf16[160,1024]{1,0:T(8,128)(2,1)} %get-tuple-element.4) | data formatting | bytes 655360

commit v3 on v2

--- a/solution.py
+++ b/solution.py
@@ -12,7 +12,8 @@
 F32 = jnp.float32
 ROWS = 160
 TAPS = 128
-UNITS = 2
+UNITS = 4
+UNIT_ROWS = 80
 ACOLS = 128
 BCOLS = 384
 
@@ -34,10 +35,10 @@
     feat_in, w_in, taps_in, filt_in, gain_in, seg_in, tgt_in, cost_in,
     out, cost_out,
     taps, filt, gain, seg_v, tgt_v, cost_v, meta, s_in, feat, qf, win, hrev, circ, mask_a, mask_b, gsend, gbuf, cbuf, slots, prevmeta,
-    packed, arrived, abuf, wa, wb, acc, osend, orecv,
+    packed, arrived, abuf, wa, wb, acc, osend, okeep,
     s_feat, s_loc, s_sib, r_sib, s_halo, r_halo, s_gx, r_gx, s_rel, r_rel, s_self,
     s_ax, r_ax, s_ay, r_ay, s_by, r_by, s_bx, r_bx, s_bx2, r_bx2,
-    s_z, r_z, s_c, r_c, s_o, r_o,
+    s_z, r_z, s_c, r_c, s_o, r_o, s_keep,
 ):
     x, y, k, z, ctx = place()
     chip = x * 8 + y
@@ -150,6 +151,7 @@
     ).astype(BF)
     win[pl.ds(288, 96), :] = jnp.zeros((96, 512), BF)
 
+    mine_rows = pl.ds(pl.multiple_of(k * ROWS, 16), ROWS)
     pl.semaphore_wait(barrier, 36)
 
     send(wcols(kk, 0, ACOLS), own_a.at[mine], s_sib.at[0], r_sib.at[0], sibling)
@@ -157,45 +159,48 @@
     send(feat.at[:, pl.ds(160, 16)], feat.at[:, pl.ds(0, 16)], s_halo.at[0], r_halo.at[0], following)
     send(meta, prevmeta, s_halo.at[1], r_halo.at[1], following)
     send(win.at[pl.ds(160, 128)], win.at[pl.ds(0, 128)], s_halo.at[2], r_halo.at[2], following)
-    tgt_row = meta[1:2, :]
-    same_target = tgt_col == tgt_row
-    rq = iota((ROWS, 256), 0)
-    rr = iota((ROWS, 256), 1)
-    rank_row = jnp.sum(jnp.where(same_target & (rq < rr), 1.0, 0.0), axis=0, keepdims=True)
-    rank_col = jnp.sum(jnp.where(same_target & (rr < rq), 1.0, 0.0), axis=1, keepdims=True)
-    kf = k.astype(F32)
-    mine_rows = pl.ds(pl.multiple_of(k * ROWS, 16), ROWS)
-    chip_row = jnp.floor(tgt_row * 0.5)
-    core_row = tgt_row - 2.0 * chip_row
-    for u in range(UNITS):
-        here = core_row == u
-        slots[k, 2 * u:2 * u + 1, :] = jnp.where(here, chip_row * 16.0 + kf * 5.0 + rank_row, -1.0)
-        slots[k, 2 * u + 1:2 * u + 2, :] = jnp.where(here, chip_row * 16.0 + 10.0, -1.0)
-    slots[k, 4:8, :] = jnp.zeros((4, 256), F32)
-    cbuf[mine_rows, :] = jnp.where(
-        iota((ROWS, 128), 1).astype(F32) == kf * 5.0 + rank_col, cost_col, 0.0
-    ).astype(BF)
-
-    flip = (iota((TAPS, TAPS), 0) + iota((TAPS, TAPS), 1)) % TAPS == 0
-    hrev[...] = jnp.dot(
-        filt[...].astype(BF), jnp.where(flip, 1.0, 0.0).astype(BF), preferred_element_type=F32
-    )
-
-    send(slots.at[k], slots.at[k], s_gx.at[1], r_gx.at[1], sibling)
-    send(cbuf.at[mine_rows], cbuf.at[mine_rows], s_gx.at[2], r_gx.at[2], sibling)
-
-    def turn(i, carry):
-        for n in range(4):
-            row = jnp.broadcast_to(hrev[pl.ds(i * 4 + n, 1), :], (TAPS, TAPS))
-            circ[i * 4 + n] = pltpu.roll(row, 0, 1, stride=1, stride_axis=0).astype(BF)
-        return carry
-
-    lax.fori_loop(0, 8, turn, 0)
-
     events = []
 
     def at(when, what, *args):
         events.append((when, len(events), functools.partial(what, *args)))
+
+    def ranks():
+        tgt_row = meta[1:2, :]
+        same_target = tgt_col == tgt_row
+        rq = iota((ROWS, 256), 0)
+        rr = iota((ROWS, 256), 1)
+        rank_row = jnp.sum(jnp.where(same_target & (rq < rr), 1.0, 0.0), axis=0, keepdims=True)
+        rank_col = jnp.sum(jnp.where(same_target & (rr < rq), 1.0, 0.0), axis=1, keepdims=True)
+        kf = k.astype(F32)
+        chip_row = jnp.floor(tgt_row * 0.5)
+        chip_col = jnp.floor(tgt_col * 0.5)
+        i_row = (tgt_row - 2.0 * chip_row) * 10.0 + kf * 5.0 + rank_row
+        i_col = (tgt_col - 2.0 * chip_col) * 10.0 + kf * 5.0 + rank_col
+        first = chip_row * 16.0
+        slots[k, 0:1, :] = jnp.where(i_row < 15.5, first + i_row, -1.0)
+        slots[k, 1:2, :] = jnp.where(i_row > 15.5, first + i_row - 16.0, -1.0)
+        slots[k, 2:3, :] = jnp.where(i_row > 15.5, first + i_row - 12.0, -1.0)
+        slots[k, 3:4, :] = first + 8.0
+        slots[k, 4:8, :] = jnp.zeros((4, 256), F32)
+        cbuf[mine_rows, :] = jnp.where(
+            iota((ROWS, 128), 1).astype(F32) == i_col, cost_col, 0.0
+        ).astype(BF)
+        send(slots.at[k], slots.at[k], s_gx.at[1], r_gx.at[1], sibling)
+        send(cbuf.at[mine_rows], cbuf.at[mine_rows], s_gx.at[2], r_gx.at[2], sibling)
+
+    def filters():
+        flip = (iota((TAPS, TAPS), 0) + iota((TAPS, TAPS), 1)) % TAPS == 0
+        hrev[...] = jnp.dot(
+            filt[...].astype(BF), jnp.where(flip, 1.0, 0.0).astype(BF), preferred_element_type=F32
+        )
+
+        def turn(i, carry):
+            for n in range(4):
+                row = jnp.broadcast_to(hrev[pl.ds(i * 4 + n, 1), :], (TAPS, TAPS))
+                circ[i * 4 + n] = pltpu.roll(row, 0, 1, stride=1, stride_axis=0).astype(BF)
+            return carry
+
+        lax.fori_loop(0, 8, turn, 0)
 
     def w_own():
         theirs = pl.ds(pl.multiple_of(kk * 64, 64), 64)
@@ -230,29 +235,32 @@
         else:
             bx_send(7)
 
-    def ay_piece(t, way):
-        ref = wa.at[(y + (1 - t if way == 0 else t - 1) + 8) % 8]
-        return ref if t < 4 else ref.at[pl.ds(way * 2, 2)]
-
-    def ay_landed(t, way):
-        ref = wa.at[(y + (-t if way == 0 else t) + 8) % 8]
-        return ref if t < 4 else ref.at[pl.ds(way * 2, 2)]
-
-    def ay_send(t):
-        for way in (0, 1):
-            piece = ay_piece(t, way)
-            send(piece, piece, s_ay.at[way, t - 1], r_ay.at[way, t - 1], dev(dy=1 - 2 * way))
+    def ay_part(off, h):
+        return wa.at[(y + off + 8) % 8, pl.ds(2 * h, 2)]
+
+    def ay_ways(t, h):
+        return (0, 1) if t < 4 else (h,)
+
+    def ay_send(t, h):
+        for way in ay_ways(t, h):
+            piece = ay_part(1 - t if way == 0 else t - 1, h)
+            send(
+                piece, piece, s_ay.at[way, t - 1, h], r_ay.at[way, t - 1, h], dev(dy=1 - 2 * way)
+            )
 
     def ax_done():
         for d in (1, 2, 3):
             arrived_at(wa.at[y, (x - d + 4) % 4], s_ax.at[d - 1], r_ax.at[d - 1])
-        ay_send(1)
+        for h in (0, 1):
+            ay_send(1, h)
 
     def ay_step(t):
-        for way in (0, 1):
-            arrived_at(ay_landed(t, way), s_ay.at[way, t - 1], r_ay.at[way, t - 1])
-        if t < 4:
-            ay_send(t + 1)
+        for h in (0, 1):
+            for way in ay_ways(t, h):
+                landed = ay_part(-t if way == 0 else t, h)
+                arrived_at(landed, s_ay.at[way, t - 1, h], r_ay.at[way, t - 1, h])
+            if t < 4:
+                ay_send(t + 1, h)
 
     def bx_row(j):
         return (y + offset_of(j) + 8) % 8
@@ -327,120 +335,147 @@
     def conv_mine():
         conv(k, gbuf, mine_rows)
 
-    totals = []
-
     def unit_rows(u):
-        return pl.ds(u * ROWS, ROWS)
-
-    def pack(u):
-        if u == 0:
-            other_rows = pl.ds(pl.multiple_of(kk * ROWS, 16), ROWS)
-            arrived_at(slots.at[kk], s_gx.at[1], r_gx.at[1])
-            arrived_at(cbuf.at[other_rows], s_gx.at[2], r_gx.at[2])
-            arrived_at(gbuf.at[other_rows], s_gx.at[0], r_gx.at[0])
+        return pl.ds(u * UNIT_ROWS, UNIT_ROWS)
+
+    own_block = pl.ds(pl.multiple_of(chip * 16, 16), 16)
+
+    def keep_own():
+        return pltpu.make_async_copy(packed.at[own_block], arrived.at[own_block], s_self)
+
+    def pack():
+        other_rows = pl.ds(pl.multiple_of(kk * ROWS, 16), ROWS)
+        arrived_at(slots.at[kk], s_gx.at[1], r_gx.at[1])
+        arrived_at(cbuf.at[other_rows], s_gx.at[2], r_gx.at[2])
+        place_row = iota((512, 2 * ROWS), 0).astype(F32)
 
         def pick(n):
             slot = jnp.concatenate([slots[0, n:n + 1, 0:ROWS], slots[1, n:n + 1, 0:ROWS]], axis=1)
-            return jnp.where(iota((512, 2 * ROWS), 0).astype(F32) == slot, 1.0, 0.0).astype(BF)
-
-        res = jnp.dot(pick(2 * u), gbuf[...], preferred_element_type=F32)
-        costs = jnp.dot(pick(2 * u + 1), cbuf[...], preferred_element_type=F32)
-        res = jnp.concatenate([res[:, 0:128] + costs, res[:, 128:256]], axis=1)
-        packed[u] = res.astype(BF)
-
-        block = pl.ds(pl.multiple_of(chip * 16, 16), 16)
-        pltpu.make_async_copy(packed.at[u, block], arrived.at[u, block], s_self.at[u]).start()
+            return jnp.where(place_row == slot, 1.0, 0.0).astype(BF)
+
+        arrived_at(gbuf.at[other_rows], s_gx.at[0], r_gx.at[0])
+        packed[:, 0:256] = jnp.dot(pick(0), gbuf[...], preferred_element_type=F32).astype(BF)
+        packed[:, 256:384] = (
+            jnp.dot(pick(1), gbuf[:, 0:128], preferred_element_type=F32)
+            + jnp.dot(pick(2), gbuf[:, 128:256], preferred_element_type=F32)
+            + jnp.dot(pick(3), cbuf[...], preferred_element_type=F32)
+        ).astype(BF)
+        keep_own().start()
 
         def post(i, carry):
-            dx = i % 4
-            dy = offset_of(i // 4)
-            other = ((x + dx) % 4) * 8 + (y + dy + 8) % 8
-            theirs = pl.ds(pl.multiple_of(other * 16, 16), 16)
+            other = ((x + i // 8 + i % 8) % 4) * 8 + (y + offset_of(7 - i % 8) + 8) % 8
             pltpu.make_async_remote_copy(
-                src_ref=packed.at[u, theirs], dst_ref=arrived.at[u, block],
-                send_sem=s_rel.at[u], recv_sem=r_rel.at[u],
+                src_ref=packed.at[pl.ds(pl.multiple_of(other * 16, 16), 16)],
+                dst_ref=arrived.at[own_block], send_sem=s_rel, recv_sem=r_rel,
                 device_id=(other * 2 + k, z), device_id_type=MESH,
             ).start()
             return carry
 
-        lax.fori_loop(1, 32, post, 0)
-
-    def relay_wait(u):
-        block = pl.ds(pl.multiple_of(chip * 16, 16), 16)
+        lax.fori_loop(0, 15, post, 0)
+        lax.fori_loop(16, 32, post, 0)
+
+    def relay_wait():
         bulk = pltpu.make_async_remote_copy(
-            src_ref=packed.at[u, pl.ds(0, 496)], dst_ref=arrived.at[u, pl.ds(0, 496)],
-            send_sem=s_rel.at[u], recv_sem=r_rel.at[u],
-            device_id=sibling, device_id_type=MESH,
+            src_ref=packed.at[pl.ds(0, 496)], dst_ref=arrived.at[pl.ds(0, 496)],
+            send_sem=s_rel, recv_sem=r_rel, device_id=sibling, device_id_type=MESH,
         )
         bulk.wait_send()
         bulk.wait_recv()
-        pltpu.make_async_copy(packed.at[u, block], arrived.at[u, block], s_self.at[u]).wait()
-
-    def unpack(u):
-        relay_wait(u)
-        pickc = jnp.where(iota((32, 512), 1) == iota((32, 512), 0) * 16 + 10, 1.0, 0.0)
-        costs = jnp.dot(pickc.astype(BF), arrived[u, :, 0:128], preferred_element_type=F32)
-        totals.append(jnp.sum(costs) / (32.0 * ROWS))
-        live = jnp.where(costs > 0.5, 1.0, 0.0)
+        keep_own().wait()
+
+    def unpack():
+        col = iota((1, 512), 1) % 16
+        spread_i = iota((128, 512), 0)
+        spread_c = iota((128, 512), 1) % 16
+        spread_a = jnp.where(spread_i == spread_c, 1.0, 0.0).astype(BF)
+        spread_b = jnp.where((spread_c < 8) & (spread_i == 16 + spread_c % 4), 1.0, 0.0).astype(BF)
+        mine_only = iota((32, 512), 0) == iota((32, 512), 1) // 16
+        pickc = jnp.where(iota((32, 512), 1) == iota((32, 512), 0) * 16 + 8, 1.0, 0.0).astype(BF)
         a = iota((128, 128), 0)
         b = iota((128, 128), 1)
-        both = (a % 5 == 0) & (a < 10) & (b < 10)
-        first = (a == 0) & (b >= 5) & (b < 10)
-        live_b = live.astype(BF)
-        tally = jnp.dot(live_b, jnp.where(both, 1.0, 0.0).astype(BF), preferred_element_type=F32)
-        before = jnp.dot(live_b, jnp.where(first, 1.0, 0.0).astype(BF), preferred_element_type=F32)
-        lower = jnp.where(iota((32, 32), 1) < iota((32, 32), 0), 1.0, 0.0)
-        rank = jnp.dot(lower.astype(BF), tally.astype(BF), preferred_element_type=F32) + before
-        code = jnp.where(live > 0.5, rank + 1.0, 0.0)
-        spread = jnp.where(iota((128, 512), 0) == iota((128, 512), 1) % 16, 1.0, 0.0)
-        wide = jnp.dot(code.astype(BF), spread.astype(BF), preferred_element_type=F32)
-        mine_only = iota((32, 512), 0) == iota((32, 512), 1) // 16
-        code_row = jnp.sum(jnp.where(mine_only, wide, 0.0), axis=0, keepdims=True)
-        i_row = iota((1, 512), 1) % 16
-        dest = (i_row % 5).astype(F32) + 5.0 * (code_row - 1.0)
-        dest = jnp.where((code_row > 0.5) & (i_row < 10), dest, -1.0)
-        hit = jnp.where(iota((ROWS, 512), 0).astype(F32) == dest, 1.0, 0.0).astype(BF)
-        rows = jnp.dot(hit, arrived[u], preferred_element_type=F32).astype(BF)
-        abuf[z * 2 + k, unit_rows(u), :] = rows
-        z_send(u, 1)
-        mine_slot = abuf.at[z * 2 + k, unit_rows(u)]
-        send(mine_slot, mine_slot, s_c.at[u, 0], r_c.at[u, 0], sibling)
+        both = (a // 10 == b // 10) & (a % 5 == 0) & (b < 20)
+        first = both & (a % 10 == 0) & (b % 10 >= 5)
+        both = jnp.where(both, 1.0, 0.0).astype(BF)
+        first = jnp.where(first, 1.0, 0.0).astype(BF)
+        lower = jnp.where(iota((32, 32), 1) < iota((32, 32), 0), 1.0, 0.0).astype(BF)
+        lane = iota((32, 128), 1)
+        relay_wait()
+        costs = jnp.dot(pickc, arrived[:, 256:384], preferred_element_type=F32)
+        mine_lane = (lane >= k * 10) & (lane < k * 10 + 10)
+        cost_out[0] = jnp.sum(jnp.where(mine_lane, costs, 0.0)) / (32.0 * ROWS)
+        live = jnp.where(costs > 0.5, 1.0, 0.0).astype(BF)
+        tally = jnp.dot(live, both, preferred_element_type=F32)
+        before = jnp.dot(live, first, preferred_element_type=F32)
+        rank = jnp.dot(lower, tally.astype(BF), preferred_element_type=F32) + before
+        code = jnp.where(costs > 0.5, rank + 1.0, 0.0).astype(BF)
+
+        def dest_row(spread, i):
+            wide = jnp.dot(code, spread, preferred_element_type=F32)
+            code_row = jnp.sum(jnp.where(mine_only, wide, 0.0), axis=0, keepdims=True)
+            dest = ((i // 10) * ROWS + i % 5).astype(F32) + 5.0 * (code_row - 1.0)
+            return jnp.where(code_row > 0.5, dest, -1.0)
+
+        dest_a = dest_row(spread_a, col)
+        dest_b = dest_row(spread_b, 16 + col % 4)
+        dest_lo = jnp.where(col < 4, dest_b, -1.0)
+        dest_hi = jnp.where(col >= 4, dest_b, -1.0)
+        target = iota((ROWS, 512), 0).astype(F32)
+        for part in range(2):
+
+            def hit(dest):
+                return jnp.where(target == dest - float(part * ROWS), 1.0, 0.0).astype(BF)
+
+            main = jnp.dot(hit(dest_a), arrived[:, 0:256], preferred_element_type=F32)
+            low = jnp.dot(hit(dest_lo), arrived[:, 256:384], preferred_element_type=F32)
+            high = jnp.dot(hit(dest_hi), arrived[:, 256:384], preferred_element_type=F32)
+            rows = jnp.concatenate([main[:, 0:128] + low, main[:, 128:256] + high], axis=1)
+            abuf[z * 2 + k, pl.ds(part * ROWS, ROWS), :] = rows.astype(BF)
+            for u in (2 * part, 2 * part + 1):
+                z_send(u, 1)
+        for u in range(UNITS):
+            mine_slot = abuf.at[z * 2 + k, unit_rows(u)]
+            send(mine_slot, mine_slot, s_c.at[u, 0], r_c.at[u, 0], sibling)
 
     def z_slot(u, off, core):
         return abuf.at[((z + off + 8) % 8) * 2 + core, unit_rows(u)]
 
-    def z_part(ref, t, way):
-        return ref if t < 4 else ref.at[pl.ds(way * 80, 80)]
+    def z_ways(u, t):
+        return (0, 1) if t < 4 else (u // 2,)
 
     def z_send(u, t):
-        for way in (0, 1):
-            piece = z_part(z_slot(u, 1 - t if way == 0 else t - 1, k), t, way)
+        for way in z_ways(u, t):
+            piece = z_slot(u, 1 - t if way == 0 else t - 1, k)
             send(piece, piece, s_z.at[u, way, t - 1], r_z.at[u, way, t - 1], dev(dz=1 - 2 * way))
 
-    def z_step(u, t):
-        for way in (0, 1):
-            landed = z_part(z_slot(u, -t if way == 0 else t, k), t, way)
-            arrived_at(landed, s_z.at[u, way, t - 1], r_z.at[u, way, t - 1])
-        if t < 4:
-            z_send(u, t + 1)
-        for j in ((2 * t - 1, 2 * t) if t < 4 else (7,)):
-            piece = z_slot(u, offset_of(j), k)
-            send(piece, piece, s_c.at[u, j], r_c.at[u, j], sibling)
+    def z_step(t, *units):
+        for u in units:
+            for way in z_ways(u, t):
+                landed = z_slot(u, -t if way == 0 else t, k)
+                arrived_at(landed, s_z.at[u, way, t - 1], r_z.at[u, way, t - 1])
+            if t < 4:
+                z_send(u, t + 1)
+            for j in ((2 * t - 1, 2 * t) if t < 4 else (7,)):
+                piece = z_slot(u, offset_of(j), k)
+                send(piece, piece, s_c.at[u, j], r_c.at[u, j], sibling)
 
     def multiply(first, last):
-        def step(j, carry):
-            zo = (z + offset_of(j) + 8) % 8
-            for u in range(UNITS):
-                arrived_at(abuf.at[zo * 2 + kk, unit_rows(u)], s_c.at[u, j], r_c.at[u, j])
-            xs = zo // 2
-            for half in (0, 1):
-                ys = (zo % 2) * 4 + 2 * half
-                part_a = jnp.concatenate([wa[ys, xs], wa[ys + 1, xs]], axis=0)
-                part_b = jnp.concatenate([wb[xs, ys], wb[xs, ys + 1]], axis=0)
-                weights = jnp.concatenate([part_a, part_b], axis=1)
-                acc[...] += jnp.dot(
-                    abuf[zo * 2 + half], weights, preferred_element_type=F32
-                )
+        def step(i, carry):
+            rows, weights = [], []
+            for n in range(2):
+                j = 2 * i + n
+                zo = (z + offset_of(j) + 8) % 8
+                for u in range(UNITS):
+                    arrived_at(abuf.at[zo * 2 + kk, unit_rows(u)], s_c.at[u, j], r_c.at[u, j])
+                xs = zo // 2
+                for half in (0, 1):
+                    rows.append(abuf[zo * 2 + half])
+                    for m in (0, 1):
+                        ys = (zo % 2) * 4 + 2 * half + m
+                        weights.append(jnp.concatenate([wa[ys, xs], wb[xs, ys]], axis=1))
+            acc[...] += jnp.dot(
+                jnp.concatenate(rows, axis=1), jnp.concatenate(weights, axis=0),
+                preferred_element_type=F32,
+            )
             return carry
 
         lax.fori_loop(first, last, step, 0)
@@ -449,56 +484,57 @@
         acc[...] = jnp.zeros_like(acc)
 
     def finish():
+        cols = pl.ds(pl.multiple_of(k * 512, 512), 512)
         theirs = pl.ds(pl.multiple_of(kk * ROWS, 16), ROWS)
-        cost_out[0] = jnp.where(k == 0, totals[0], totals[1])
         osend[...] = acc[theirs, :].astype(BF)
-        send(osend, orecv, s_o, r_o, sibling)
-        out[:, pl.ds(pl.multiple_of(k * 512, 512), 512)] = acc[mine_rows, :].astype(BF)
-        arrived_at(orecv, s_o, r_o)
-        out[:, pl.ds(pl.multiple_of(kk * 512, 512), 512)] = orecv[...]
+        send(osend, out.at[:, cols], s_o, r_o, sibling)
+        okeep[...] = acc[mine_rows, :].astype(BF)
+        keep = pltpu.make_async_copy(okeep, out.at[:, cols], s_keep)
+        keep.start()
+        keep.wait()
+        arrived_at(out.at[:, pl.ds(pl.multiple_of(kk * 512, 512), 512)], s_o, r_o)
 
     plan = (
         (w_own, 1),
-        (halo, 2),
-        (conv_theirs, 3),
-        (ax_done, 4),
-        (by_step, 5, 1),
-        (by_send, 6, 2),
-        (conv_mine, 7),
-        (pack, 8, 0),
-        (pack, 9, 1),
-        (clear, 10),
+        (ranks, 2),
+        (filters, 3),
+        (halo, 4),
+        (conv_theirs, 5),
+        (conv_mine, 6),
+        (by_step, 7, 1),
+        (by_send, 8, 2),
+        (pack, 9),
+        (ax_done, 10),
         (bx_step, 11, 0),
         (by_step, 12, 2),
-        (bx_step, 13, 1),
-        (bx_step, 14, 2),
-        (unpack, 15, 0),
-        (by_send, 16, 3),
-        (unpack, 17, 1),
-        (ay_step, 18, 1),
-        (z_step, 19, 0, 1),
-        (by_step, 20, 3),
-        (by_send, 21, 4),
-        (bx_step, 22, 3),
-        (bx_step, 23, 4),
-        (z_step, 24, 1, 1),
+        (by_send, 13, 3),
+        (bx_step, 14, 1),
+        (bx_step, 15, 2),
+        (clear, 16),
+        (unpack, 17),
+        (bx_step, 18, 3),
+        (bx_step, 19, 4),
+        (ay_step, 20, 1),
+        (by_step, 21, 3),
+        (by_send, 22, 4),
+        (z_step, 23, 1, 0, 1),
+        (z_step, 24, 1, 2, 3),
         (ay_step, 25, 2),
-        (z_step, 26, 0, 2),
-        (by_step, 27, 4),
-        (bx_step, 28, 5),
-        (z_step, 29, 1, 2),
-        (bx_step, 30, 6),
+        (by_step, 26, 4),
+        (bx_step, 27, 5),
+        (bx_step, 28, 6),
+        (z_step, 29, 2, 0, 1),
+        (z_step, 30, 2, 2, 3),
         (ay_step, 31, 3),
-        (z_step, 32, 0, 3),
-        (bx_step, 33, 7),
-        (z_step, 34, 1, 3),
-        (ay_step, 35, 4),
-        (w_last, 36),
-        (multiply, 37, 0, 5),
-        (z_step, 38, 0, 4),
-        (z_step, 39, 1, 4),
-        (multiply, 40, 5, 8),
-        (finish, 41),
+        (bx_step, 32, 7),
+        (z_step, 33, 3, 0, 1),
+        (z_step, 34, 3, 2, 3),
+        (z_step, 35, 4, 0, 1),
+        (z_step, 36, 4, 2, 3),
+        (ay_step, 37, 4),
+        (w_last, 38),
+        (multiply, 39, 0, 4),
+        (finish, 40),
     )
     for what, when, *args in plan:
         at(when, what, *args)
@@ -522,7 +558,7 @@
             jax.ShapeDtypeStruct((1,), F32),
         ),
         in_specs=[hbm] * 8,
-        out_specs=(vmem, pl.BlockSpec(memory_space=pltpu.SMEM)),
+        out_specs=(hbm, pl.BlockSpec(memory_space=pltpu.SMEM)),
         scratch_shapes=[
             pltpu.VMEM((3, 3, 512), F32),
             pltpu.VMEM((32, TAPS), F32),
@@ -544,8 +580,8 @@
             pltpu.VMEM((2 * ROWS, 128), BF),
             pltpu.VMEM((2, 8, 256), F32),
             pltpu.VMEM((8, 256), F32),
-            pltpu.VMEM((u, 512, 256), BF),
-            pltpu.VMEM((u, 512, 256), BF),
+            pltpu.VMEM((512, 384), BF),
+            pltpu.VMEM((512, 384), BF),
             pltpu.VMEM((16, 2 * ROWS, 256), BF),
             pltpu.VMEM((8, 4, 128, ACOLS), BF),
             pltpu.VMEM((4, 8, 128, BCOLS), BF),
@@ -553,10 +589,10 @@
             pltpu.VMEM((ROWS, 512), BF),
             pltpu.VMEM((ROWS, 512), BF),
             dma, dma((2,)), dma((2,)), dma((2,)), dma((3,)), dma((3,)), dma((3,)), dma((3,)),
-            dma((u,)), dma((u,)), dma((u,)),
-            dma((3,)), dma((3,)), dma((2, 4)), dma((2, 4)), dma((2, 4)), dma((2, 4)),
+            dma, dma, dma,
+            dma((3,)), dma((3,)), dma((2, 4, 2)), dma((2, 4, 2)), dma((2, 4)), dma((2, 4)),
             dma((2, 8)), dma((2, 8)), dma((8,)), dma((8,)),
-            dma((u, 2, 4)), dma((u, 2, 4)), dma((u, 8)), dma((u, 8)), dma, dma,
+            dma((u, 2, 4)), dma((u, 2, 4)), dma((u, 8)), dma((u, 8)), dma, dma, dma,
         ],
         compiler_params=pltpu.CompilerParams(
             collective_id=0, has_side_effects=True, vmem_limit_bytes=60 * 2**20

time: 68.8 us -> 66.6 us (0.968)
  Pallas kernels: 64.5 us -> 62.4 us
    pallas_call x1, Pallas kernels: 64.5 us -> 62.4 us  [local(): pl.pallas_call(mixer_kernel, out_shape=(jax.ShapeDtypeStruct((ROWS, 1024)...]
where the time goes in v3:
time: 66.6 us; the launch traced here: 66.5 us
  Pallas kernels  62.4 us (94%)
  between operations  2.33 us (3%)
  local copies, waits for them, and re-layouts  1.72 us (3%)
    pallas_call x1, Pallas kernels, local(): pl.pallas_call(mixer_kernel, out_shape=(jax.ShapeDtypeStruct((ROWS, 1024)...  62.4 us
    unnamed x1, local copies, waits for them, and re-layouts  1.72 us

profile of v3, /device:TPU:1, one launch (start us, length us, event | category | flops | bytes accessed | tf_op | source)
XLA Modules:
  0.0 66.5 jit_solution(16671652050070667720)
XLA Ops:
  0.6 62.4 %mixer.1 = (bf16[160,1024]{1,0:T(8,128)(2,1)}, f32[1]{0:T(128)}) custom-call(bf16[3,160,512]{2,1,0:T(8,128)(2,1)} %bitcast.5, bf16[64,1024]{1,0:T(8,128)(2,1)} %w_in.1, f32[3,3,512]{2,1,0:T(4,128)} %taps_in.1, f32[32,128]{1,0:T(8,128)} %filt_in.1, f32[1,512]{1,0:T(1,128)} %bitcast.6, s32[1,160]{1,0:T(1,128)} %bitcast.7, s32[1,160]{1,0:T(1,128)} %bitcast.8, ...), custom_call_target="tpu_custom_call" | custom-call | flops 1342177280 | bytes 16777216 | tf_op jit(solution)/shard_map/mixer/pallas_call | solution.py:554
  63.0 1.7 %copy.12 = bf16[160,1024]{1,0:T(8,128)(2,1)} copy(bf16[160,1024]{1,0:T(8,128)(2,1)} %get-tuple-element.4) | data formatting | bytes 655360

commit v4 on v3

--- a/solution.py
+++ b/solution.py
@@ -458,27 +458,29 @@
                 piece = z_slot(u, offset_of(j), k)
                 send(piece, piece, s_c.at[u, j], r_c.at[u, j], sibling)
 
-    def multiply(first, last):
+    def multiply(part, wait):
+        part_rows = pl.ds(pl.multiple_of(part * ROWS, 16), ROWS)
+
         def step(i, carry):
             rows, weights = [], []
             for n in range(2):
                 j = 2 * i + n
                 zo = (z + offset_of(j) + 8) % 8
-                for u in range(UNITS):
+                for u in range(UNITS if wait else 0):
                     arrived_at(abuf.at[zo * 2 + kk, unit_rows(u)], s_c.at[u, j], r_c.at[u, j])
                 xs = zo // 2
                 for half in (0, 1):
-                    rows.append(abuf[zo * 2 + half])
+                    rows.append(abuf[zo * 2 + half, part_rows, :])
                     for m in (0, 1):
                         ys = (zo % 2) * 4 + 2 * half + m
                         weights.append(jnp.concatenate([wa[ys, xs], wb[xs, ys]], axis=1))
-            acc[...] += jnp.dot(
+            acc[part_rows, :] += jnp.dot(
                 jnp.concatenate(rows, axis=1), jnp.concatenate(weights, axis=0),
                 preferred_element_type=F32,
             )
             return carry
 
-        lax.fori_loop(first, last, step, 0)
+        lax.fori_loop(0, 4, step, 0)
 
     def clear():
         acc[...] = jnp.zeros_like(acc)
@@ -486,8 +488,10 @@
     def finish():
         cols = pl.ds(pl.multiple_of(k * 512, 512), 512)
         theirs = pl.ds(pl.multiple_of(kk * ROWS, 16), ROWS)
+        multiply(kk, True)
         osend[...] = acc[theirs, :].astype(BF)
         send(osend, out.at[:, cols], s_o, r_o, sibling)
+        multiply(k, False)
         okeep[...] = acc[mine_rows, :].astype(BF)
         keep = pltpu.make_async_copy(okeep, out.at[:, cols], s_keep)
         keep.start()
@@ -519,22 +523,21 @@
         (by_send, 22, 4),
         (z_step, 23, 1, 0, 1),
         (z_step, 24, 1, 2, 3),
-        (ay_step, 25, 2),
-        (by_step, 26, 4),
-        (bx_step, 27, 5),
-        (bx_step, 28, 6),
-        (z_step, 29, 2, 0, 1),
+        (by_step, 25, 4),
+        (ay_step, 26, 2),
+        (z_step, 27, 2, 0, 1),
+        (bx_step, 28, 5),
+        (bx_step, 29, 6),
         (z_step, 30, 2, 2, 3),
-        (ay_step, 31, 3),
-        (bx_step, 32, 7),
+        (bx_step, 31, 7),
+        (ay_step, 32, 3),
         (z_step, 33, 3, 0, 1),
         (z_step, 34, 3, 2, 3),
         (z_step, 35, 4, 0, 1),
         (z_step, 36, 4, 2, 3),
         (ay_step, 37, 4),
         (w_last, 38),
-        (multiply, 39, 0, 4),
-        (finish, 40),
+        (finish, 39),
     )
     for what, when, *args in plan:
         at(when, what, *args)

time: 66.6 us -> 66.1 us (level)
  no operation moved by 1% of the time
where the time goes in v4:
time: 66.1 us; the launch traced here: 65.9 us
  Pallas kernels  61.8 us (93%)
  between operations  2.33 us (4%)
  local copies, waits for them, and re-layouts  1.72 us (3%)
    pallas_call x1, Pallas kernels, local(): pl.pallas_call(mixer_kernel, out_shape=(jax.ShapeDtypeStruct((ROWS, 1024)...  61.8 us
    unnamed x1, local copies, waits for them, and re-layouts  1.72 us

profile of v4, /device:TPU:1, one launch (start us, length us, event | category | flops | bytes accessed | tf_op | source)
XLA Modules:
  0.0 65.9 jit_solution(12894943292577248065)
XLA Ops:
  0.6 61.8 %mixer.1 = (bf16[160,1024]{1,0:T(8,128)(2,1)}, f32[1]{0:T(128)}) custom-call(bf16[3,160,512]{2,1,0:T(8,128)(2,1)} %bitcast.5, bf16[64,1024]{1,0:T(8,128)(2,1)} %w_in.1, f32[3,3,512]{2,1,0:T(4,128)} %taps_in.1, f32[32,128]{1,0:T(8,128)} %filt_in.1, f32[1,512]{1,0:T(1,128)} %bitcast.6, s32[1,160]{1,0:T(1,128)} %bitcast.7, s32[1,160]{1,0:T(1,128)} %bitcast.8, ...), custom_call_target="tpu_custom_call" | custom-call | flops 1342177280 | bytes 16777216 | tf_op jit(solution)/shard_map/mixer/pallas_call | solution.py:557
  62.5 1.7 %copy.12 = bf16[160,1024]{1,0:T(8,128)(2,1)} copy(bf16[160,1024]{1,0:T(8,128)(2,1)} %get-tuple-element.4) | data formatting | bytes 655360
